TPU v7x, 32 devices: a whole 2x2x4 slice. The times are simulated.
32 devices in a mesh: ctx: 8 (over z, x), head: 4 (over y, core).
Axes of the slice: x: 2, y: 2, z: 4, core: 2. Of those that a mesh axis runs over, the one named last changes fastest.
Arguments:
- lin_query: bfloat16 [1024, 8192], P('ctx', 'head'), may hold values from -6 to 6
- lin_key: bfloat16 [1024, 8192], P('ctx', 'head'), may hold values from -6 to 6
- lin_value: bfloat16 [1024, 8192], P('ctx', 'head'), may hold values from -6 to 6
- log_decay: float32 [1024, 64], P('ctx', 'head'), may hold values from -1 to 0, as said below
- soft_query: bfloat16 [1024, 8192], P('ctx', 'head'), may hold values from -24 to 24
- soft_key: bfloat16 [1024, 8192], P('ctx', 'head'), may hold values from -24 to 24
- soft_value: bfloat16 [1024, 8192], P('ctx', 'head'), may hold values from -6 to 6
Outputs:
- lin_out: bfloat16 [1024, 8192], P('ctx', 'head')
- soft_out: bfloat16 [1024, 8192], P('ctx', 'head')
Inputs may be any that keep to these rules, and one draw needn't show every extreme that they name: `log_decay`: never positive.
All inputs are finite; a program needn't handle non-finite values.
Results may differ from a plain program's by a relative error of at most 0.0065.
Values may be sent and summed in bfloat16 or wider, within the bound.
A program may use at most 192 MiB of HBM per device.

v0:
```python
import jax
import jax.numpy as jnp
from jax import lax
from jax.sharding import PartitionSpec as P

HEAD_DIM = 128


norm_eps = 1e-06
masked_score = -1e30
key_span = 512
query_span = 512


def entering(value, axis, join, neutral):
    count, mine = (lax.axis_size(axis), lax.axis_index(axis))
    pieces = jax.tree.map(lambda part: lax.all_gather(part, axis), value)
    subtotal = jax.tree.map(
        lambda part, zero: jnp.full_like(part, 0) + jnp.asarray(zero, part.dtype), value, neutral
    )

    def step(position, subtotal):
        longer = join(subtotal, jax.tree.map(lambda part: part[position], pieces))
        return jax.tree.map(lambda new, old: jnp.where(position < mine, new, old), longer, subtotal)

    return lax.fori_loop(0, count - 1, step, subtotal)


def merge_states(earlier, later):
    decay_early, state_early = earlier
    decay_late, state_late = later
    return (decay_early * decay_late, decay_late[:, None, None] * state_early + state_late)


def lightning_core(lin_query, lin_key, lin_value, log_decay):
    tokens = lin_query.shape[0]
    heads_here = log_decay.shape[1]
    query_heads = lin_query.reshape(tokens, heads_here, HEAD_DIM)
    key_heads = lin_key.reshape(tokens, heads_here, HEAD_DIM)
    value_heads = lin_value.reshape(tokens, heads_here, HEAD_DIM)
    running_sum = jnp.cumsum(log_decay, axis=0)
    ending = running_sum[-1]
    scores = jnp.einsum("thd,shd->hts", query_heads, key_heads, preferred_element_type=jnp.float32)
    causal = jnp.arange(tokens)[:, None] >= jnp.arange(tokens)[None, :]
    spread = running_sum.T[:, :, None] - running_sum.T[:, None, :]
    decayed = (
        jnp.where(causal[None], jnp.exp(jnp.where(causal[None], spread, 0.0)), 0.0) * scores
    ).astype(jnp.bfloat16)
    inside = jnp.einsum("hts,shd->thd", decayed, value_heads, preferred_element_type=jnp.float32)
    to_end = jnp.exp(ending[None, :] - running_sum)
    key_scaled = (key_heads.astype(jnp.float32) * to_end[:, :, None]).astype(jnp.bfloat16)
    block_state = jnp.einsum(
        "shd,she->hde", key_scaled, value_heads, preferred_element_type=jnp.float32
    )
    block_decay = jnp.exp(ending)
    before = entering(
        (block_decay, block_state),
        "ctx",
        merge_states,
        (jnp.ones_like(block_decay), jnp.zeros_like(block_state)),
    )
    prior_state = before[1]
    query_scaled = (query_heads.astype(jnp.float32) * jnp.exp(running_sum)[:, :, None]).astype(
        jnp.bfloat16
    )
    outside = jnp.einsum(
        "thd,hde->the",
        query_scaled,
        prior_state.astype(jnp.bfloat16),
        preferred_element_type=jnp.float32,
    )
    total = inside + outside
    normed = total * lax.rsqrt(jnp.mean(total * total, axis=-1, keepdims=True) + norm_eps)
    return normed.reshape(tokens, heads_here * HEAD_DIM).astype(jnp.bfloat16)


def prepare_queries(query_mine, tokens, quarter, head_slot):
    rows_all = query_mine.shape[0]
    heads_now = query_mine.shape[1] // HEAD_DIM
    tile_rows = query_span if rows_all % query_span == 0 else rows_all
    blocks_count = rows_all // tile_rows
    query_blocks = query_mine.reshape(blocks_count, tile_rows, heads_now, HEAD_DIM)
    index_all = jnp.arange(rows_all, dtype=jnp.int32)
    token_slots = index_all // quarter * tokens + head_slot * quarter + index_all % quarter
    initial = (
        jnp.full((blocks_count, tile_rows, heads_now), masked_score, jnp.float32),
        jnp.zeros((blocks_count, tile_rows, heads_now), jnp.float32),
        jnp.zeros((blocks_count, tile_rows, heads_now, HEAD_DIM), jnp.float32),
    )
    return (query_blocks, token_slots.reshape(blocks_count, tile_rows), initial)


def attend_keys(carry, query_blocks, query_places, keys_flat, values_flat, key_places):
    key_total = keys_flat.shape[0]
    heads_now = query_blocks.shape[2]
    keys_heads = keys_flat.reshape(key_total, heads_now, HEAD_DIM)
    values_heads = values_flat.reshape(key_total, heads_now, HEAD_DIM)
    score_scale = HEAD_DIM ** (-0.5)

    def per_block(packed):
        best_start, mass_start, accum_start, query_tile, query_where = packed
        latest_query = jnp.max(query_where)

        def per_span(span_index, running):
            start_row = span_index * key_span
            key_where = lax.dynamic_slice_in_dim(key_places, start_row, key_span, 0)

            def compute(state_now):
                best_now, mass_now, accum_now = state_now
                key_tile = lax.dynamic_slice_in_dim(keys_heads, start_row, key_span, 0)
                value_tile = lax.dynamic_slice_in_dim(values_heads, start_row, key_span, 0)
                scores = (
                    jnp.einsum(
                        "qhd,khd->qhk", query_tile, key_tile, preferred_element_type=jnp.float32
                    )
                    * score_scale
                )
                allowed = (key_where[None, :] <= query_where[:, None])[:, None, :]
                scores = jnp.where(allowed, scores, masked_score)
                best_next = jnp.maximum(best_now, jnp.max(scores, axis=-1))
                expo = jnp.where(allowed, jnp.exp(scores - best_next[:, :, None]), 0.0)
                shrink = jnp.exp(best_now - best_next)
                mass_next = mass_now * shrink + jnp.sum(expo, axis=-1)
                accum_next = accum_now * shrink[:, :, None] + jnp.einsum(
                    "qhk,khd->qhd",
                    expo.astype(jnp.bfloat16),
                    value_tile,
                    preferred_element_type=jnp.float32,
                )
                return (best_next, mass_next, accum_next)

            def unchanged(state_now):
                return state_now

            return lax.cond(jnp.min(key_where) <= latest_query, compute, unchanged, running)

        return lax.fori_loop(
            0, key_total // key_span, per_span, (best_start, mass_start, accum_start)
        )

    return lax.map(per_block, (carry[0], carry[1], carry[2], query_blocks, query_places))


def softmax_core(soft_query, soft_key, soft_value):
    tokens = soft_query.shape[0]
    quarter = tokens // lax.axis_size("head")
    head_slot = lax.axis_index("head")
    query_moved, key_moved, value_moved = (
        lax.all_to_all(soft_query, "head", split_axis=0, concat_axis=1, tiled=True),
        lax.all_to_all(soft_key, "head", split_axis=0, concat_axis=1, tiled=True),
        lax.all_to_all(soft_value, "head", split_axis=0, concat_axis=1, tiled=True),
    )
    query_mine, key_mine, value_mine = (
        lax.all_to_all(query_moved, "ctx", split_axis=1, concat_axis=0, tiled=True),
        lax.all_to_all(key_moved, "ctx", split_axis=1, concat_axis=0, tiled=True),
        lax.all_to_all(value_moved, "ctx", split_axis=1, concat_axis=0, tiled=True),
    )
    query_blocks, query_places, initial = prepare_queries(query_mine, tokens, quarter, head_slot)
    resident_rows = key_mine.shape[0]
    pieces = (
        lax.all_gather(key_mine, "head", axis=0, tiled=True),
        lax.all_gather(value_mine, "head", axis=0, tiled=True),
    )
    key_total = pieces[0].shape[0]
    index_all = jnp.arange(key_total, dtype=jnp.int32)
    source = index_all // resident_rows
    within = index_all % resident_rows
    token_slots = within // quarter * tokens + source * quarter + within % quarter
    result = attend_keys(initial, query_blocks, query_places, pieces[0], pieces[1], token_slots)
    best_final, mass_final, accum_final = result
    outcome = (
        (accum_final / mass_final[..., None]).reshape(query_mine.shape[0], -1).astype(jnp.bfloat16)
    )
    return lax.all_to_all(
        lax.all_to_all(outcome, "ctx", split_axis=0, concat_axis=1, tiled=True),
        "head",
        split_axis=1,
        concat_axis=0,
        tiled=True,
    )


def shards(lin_query, lin_key, lin_value, log_decay, soft_query, soft_key, soft_value):
    lin_out = lightning_core(lin_query, lin_key, lin_value, log_decay)
    soft_out = softmax_core(soft_query, soft_key, soft_value)
    return (lin_out, soft_out)


def solution(mesh):
    in_specs = (
        P("ctx", "head"),
        P("ctx", "head"),
        P("ctx", "head"),
        P("ctx", "head"),
        P("ctx", "head"),
        P("ctx", "head"),
        P("ctx", "head"),
    )
    out_specs = (P("ctx", "head"), P("ctx", "head"))
    return jax.shard_map(shards, mesh=mesh, in_specs=in_specs, out_specs=out_specs, check_vma=False)
```

profile of v0, /device:TPU:0, one launch (start us, length us, event | category | flops | bytes accessed | tf_op | source)
XLA Modules:
  0.0 248.8 jit_solution(2099448249604024288)
XLA Ops:
  7.2 13.2 %all_to_all.134 = bf16[4,32,2048]{2,1,0:T(8,128)(2,1)S(1)} all-to-all(bf16[4,32,2048]{2,1,0:T(8,128)(2,1)} %bitcast.116), channel_id=1, replica_groups=mesh['ctx'=8,'head'=4] {'head'}, dimensions={0} | all-to-all | bytes 1048576 | tf_op jit(solution)/shard_map/all_to_all | solution.py:150
  21.3 20.6 %all_to_all.135 = bf16[32,8,1024]{2,0,1:T(8,128)(2,1)} all-to-all(bf16[32,8,1024]{2,0,1:T(8,128)(2,1)S(1)} %copy.86), channel_id=1, replica_groups=mesh['ctx'=8,'head'=4] {'ctx'}, dimensions={1} | all-to-all | bytes 1048576 | tf_op jit(solution)/shard_map/all_to_all | solution.py:155
  42.0 14.6 %all_to_all.136 = bf16[4,32,2048]{2,1,0:T(8,128)(2,1)S(1)} all-to-all(bf16[4,32,2048]{2,1,0:T(8,128)(2,1)S(1)} %bitcast.117), channel_id=1, replica_groups=mesh['ctx'=8,'head'=4] {'head'}, dimensions={0} | all-to-all | bytes 1048576 | tf_op jit(solution)/shard_map/all_to_all | solution.py:151
  56.6 0.4 copy.90
  57.4 17.2 %all_to_all.137 = bf16[32,8,1024]{2,0,1:T(8,128)(2,1)} all-to-all(bf16[32,8,1024]{2,0,1:T(8,128)(2,1)S(1)} %copy.91), channel_id=1, replica_groups=mesh['ctx'=8,'head'=4] {'ctx'}, dimensions={1} | all-to-all | bytes 1048576 | tf_op jit(solution)/shard_map/all_to_all | solution.py:156
  75.4 1.3 fusion.34
  76.7 16.9 %all_to_all.138 = bf16[4,32,2048]{2,1,0:T(8,128)(2,1)S(1)} all-to-all(bf16[4,32,2048]{2,1,0:T(8,128)(2,1)S(1)} %bitcast.118), channel_id=1, replica_groups=mesh['ctx'=8,'head'=4] {'head'}, dimensions={0} | all-to-all | bytes 1048576 | tf_op jit(solution)/shard_map/all_to_all | solution.py:149
  94.1 1.1 copy.89
  95.2 3.5 %all-to-all-start.3 = ((bf16[32,8,1024]{2,0,1:T(8,128)(2,1)}), bf16[32,8,1024]{2,0,1:T(8,128)(2,1)S(1)}, u32[]{:S(2)}, u32[]{:S(2)}) async-start(bf16[32,8,1024]{2,0,1:T(8,128)(2,1)} %copy.89), calls=%async_computation.3 | async-start | bytes 1048576 | tf_op jit(solution)/shard_map/all_to_all | solution.py:154
  98.7 0.7 fusion.75
  99.4 13.5 %all-to-all-done.3 = bf16[32,8,1024]{2,0,1:T(8,128)(2,1)S(1)} async-done(((bf16[32,8,1024]{2,0,1:T(8,128)(2,1)}), bf16[32,8,1024]{2,0,1:T(8,128)(2,1)S(1)}, u32[]{:S(2)}, u32[]{:S(2)}) %all-to-all-start.3) | async-done | bytes 524320 | tf_op jit(solution)/shard_map/all_to_all | solution.py:154
  113.1 4.0 %copy.87 = bf16[1024,1024]{0,1:T(8,128)(2,1)} copy(bf16[1024,1024]{1,0:T(8,128)(2,1)} %all-gather.6.cloned.1.call-done) | data formatting | bytes 4194304 | tf_op jit(solution)/shard_map/all_gather | solution.py:161
  117.0 3.0 %copy.92 = bf16[1024,8,128]{2,0,1:T(8,128)(2,1)S(1)} copy(bf16[1024,8,128]{0,2,1:T(8,128)(2,1)} %bitcast.100) | data formatting | bytes 4194304
  120.1 4.0 %copy.101 = bf16[1024,1024]{0,1:T(8,128)(2,1)} copy(bf16[1024,1024]{1,0:T(8,128)(2,1)} %all-gather.8.cloned.1.call-done) | data formatting | bytes 4194304
  124.1 1.1 squeeze.35
  125.1 13.3 %while.41 = (s32[]{:T(128)}, f32[256,8]{0,1:T(8,128)S(1)}, f32[256,8]{0,1:T(8,128)S(1)}, f32[256,8,128]{0,2,1:T(8,128)}, s32[1024]{0:T(1024)S(1)}, /*index=5*/s3...) while((s32[]{:T(128)}, f32[256,8]{0,1:T(8,128)S(1)}, ...), condition=%wide.region_11.12_spmd.clone, body=%wide.region_5.11_spmd.clone.sunk | while | flops 551166464 | bytes 34754596 | solution.py:137
  125.1 0.8 fusion.86
  127.3 4.5 %conditional.3 = ((f32[256,8]{0,1:T(8,128)S(1)}, f32[256,8]{0,1:T(8,128)S(1)}, f32[256,8,128]{0,2,1:T(8,128)})) conditional(s32[]{:T(128)} %convert_element_type.81, (f32[256,8]{0,1:T(8,128)S(1)}, f32[256,8]{0,1:T(8,128)S(1)}, f32[256,8,128]{0,2,1:T(8,128)}) %tuple.109, (s32[512]{0:T(512)S(1)}, s32[256]{0:T(256)S(1)}, s32[]{:T(128)}, ...), branch_computations={%region_7.7_spmd, %region_8.10_spmd.clone} | conditional | flops 551164928 | bytes 34745768 | solution.py:135
  127.5 0.8 fusion.3
  128.3 1.0 fusion.5
  129.4 1.4 fusion.12
  130.8 1.0 copy-done.2
  131.8 0.8 fusion.86
  133.9 4.5 %conditional.3 = ((f32[256,8]{0,1:T(8,128)S(1)}, f32[256,8]{0,1:T(8,128)S(1)}, f32[256,8,128]{0,2,1:T(8,128)})) conditional(s32[]{:T(128)} %convert_element_type.81, (f32[256,8]{0,1:T(8,128)S(1)}, f32[256,8]{0,1:T(8,128)S(1)}, f32[256,8,128]{0,2,1:T(8,128)}) %tuple.109, (s32[512]{0:T(512)S(1)}, s32[256]{0:T(256)S(1)}, s32[]{:T(128)}, ...), branch_computations={%region_7.7_spmd, %region_8.10_spmd.clone} | conditional | flops 551164928 | bytes 34745768 | solution.py:135
  134.1 0.8 fusion.3
  134.9 1.0 fusion.5
  136.1 1.4 fusion.12
  137.5 1.0 copy-done.2
  138.5 1.4 divide_convert_fusion
  140.2 1.0 convert_element_type.50
  141.2 3.6 %all-to-all-start.6 = ((bf16[8,32,1024]{2,1,0:T(8,128)(2,1)}), bf16[8,32,1024]{2,1,0:T(8,128)(2,1)S(1)}, u32[]{:S(2)}, u32[]{:S(2)}) async-start(bf16[8,32,1024]{2,1,0:T(8,128)(2,1)} %convert_element_type.50), calls=%async_computation.6 | async-start | bytes 1048576 | tf_op jit(solution)/shard_map/all_to_all | solution.py:175
  144.9 23.2 %all-gather.1 = f32[8,1,16]{2,1,0:T(1,128)S(1)} all-gather(f32[1,1,16]{2,1,0:T(1,128)S(1)} %get-tuple-element.537), channel_id=1, replica_groups=mesh['ctx'=8,'head'=4] {'ctx'}, dimensions={0}, use_global_device_ids=true | all-gather | bytes 576 | tf_op jit(solution)/shard_map/all_gather | solution.py:17
  168.9 1.1 copy.97
  170.0 3.5 %all-to-all-start.7 = ((bf16[32,4,2048]{2,0,1:T(8,128)(2,1)}), bf16[32,4,2048]{2,0,1:T(8,128)(2,1)S(1)}, u32[]{:S(2)}, u32[]{:S(2)}) async-start(bf16[32,4,2048]{2,0,1:T(8,128)(2,1)} %copy.97), calls=%async_computation.7 | async-start | bytes 1048576 | tf_op jit(solution)/shard_map/all_to_all | solution.py:174
  173.6 2.9 %convolution_bitcast_fusion.1 = f32[128,16,128]{0,2,1:T(8,128)} fusion(bf16[128,16,128]{0,2,1:T(8,128)(2,1)S(1)} %bitcast.114, f32[16,128]{1,0:T(8,128)S(1)} %copy.74, pred[128,128]{1,0:T(8,128)(4,1)S(1)} %iota_compare_fusion, bf16[128,2048]{1,0:T(8,128)(2,1)} %param.15, bf16[128,2048]{1,0:T(8,128)(2,1)S(1)} %copy-done), kind=kOutput, calls=%fused_computation.36 | convolution fusion | flops 135528448 | bytes 2646016 | tf_op jit(solution)/shard_map/hts,shd->thd/dot_general | solution.py:49
  176.4 5.9 %all-to-all-done.7 = bf16[32,4,2048]{2,0,1:T(8,128)(2,1)S(1)} async-done(((bf16[32,4,2048]{2,0,1:T(8,128)(2,1)}), bf16[32,4,2048]{2,0,1:T(8,128)(2,1)S(1)}, u32[]{:S(2)}, u32[]{:S(2)}) %all-to-all-start.7) | async-done | bytes 524320 | tf_op jit(solution)/shard_map/all_to_all | solution.py:174
  182.3 46.4 %all-gather.10.cloned.1.call-done = f32[128,128,128]{2,1,0:T(8,128)} async-done(((f32[16,128,128]{2,1,0:T(8,128)}), f32[128,128,128]{2,1,0:T(8,128)}) %all-gather.10.cloned.1.call-update) | async-done | bytes 8388624 | tf_op jit(solution)/shard_map/all_gather | solution.py:17
  228.8 10.6 %while.42 = (s32[]{:T(128)}, f32[16,128,128]{2,1,0:T(8,128)S(1)}, s32[]{:T(128)}, f32[8,16]{1,0:T(8,128)S(1)}, f32[8,16,128,128]{3,2,1,0:T(8,128)}, /*index=5*/s32[]{:T(128)}, s32[]{:T(128)}) while((s32[]{:T(128)}, f32[16,128,128]{2,1,0:T(8,128)S(1)}, s32[]{:T(128)}, f32[8,16]{1,0:T(8,128)S(1)}, f32[8,16,128,128]{3,2,1,0:T(8,128)}, ...), condition=%wide.region_2.3_spmd.clone, body=%wide.region_1.2_spmd.clone.sunk | while | flops 1048580 | bytes 3146033 | solution.py:26
  228.8 1.5 fusion.87
  230.4 1.5 fusion.87
  231.9 1.5 fusion.87
  233.4 1.5 fusion.87
  234.9 1.5 fusion.87
  236.4 1.5 fusion.87
  237.9 1.5 fusion.87
  239.3 1.0 multiply_reduce_fusion
  240.4 1.0 copy.98
  241.4 0.8 copy.150
  (89 shorter events, 4.8 us)
Async XLA Ops:
  7.2 166.4 %copy-start = (bf16[128,2048]{1,0:T(8,128)(2,1)S(1)}, bf16[128,2048]{1,0:T(8,128)(2,1)}, u32[]{:S(2)}) copy-start(bf16[128,2048]{1,0:T(8,128)(2,1)} %param.13) | copy-start | bytes 1572868
  7.2 34.8 %copy-start.7 = (bf16[128,2048]{1,0:T(8,128)(2,1)S(1)}, bf16[128,2048]{1,0:T(8,128)(2,1)}, u32[]{:S(2)}) copy-start(bf16[128,2048]{1,0:T(8,128)(2,1)} %param.19) | copy-start | bytes 1572868
  7.2 105.9 %all-gather.6.cloned.1.call-start = ((), (), s32[]{:S(2)}) async-start(), calls=%async_computation.8 | async-start | bytes 2621440 | tf_op jit(solution)/shard_map/all_gather | solution.py:161
  21.0 53.7 %copy-start.8 = (bf16[128,2048]{1,0:T(8,128)(2,1)S(1)}, bf16[128,2048]{1,0:T(8,128)(2,1)}, u32[]{:S(2)}) copy-start(bf16[128,2048]{1,0:T(8,128)(2,1)} %param.14) | copy-start | bytes 1572868
  21.3 53.7 %copy-start.11 = (f32[128,16]{0,1:T(8,128)S(1)}, f32[128,16]{0,1:T(8,128)}, u32[]{:S(2)}) copy-start(f32[128,16]{0,1:T(8,128)} %param.16) | copy-start | bytes 24580
  21.3 54.0 %copy-start.10 = (bf16[128,2048]{1,0:T(8,128)(2,1)S(1)}, bf16[128,2048]{1,0:T(8,128)(2,1)}, u32[]{:S(2)}) copy-start(bf16[128,2048]{1,0:T(8,128)(2,1)} %param.15) | copy-start | bytes 1572868
  42.0 78.1 %all-gather.8.cloned.1.call-start = ((), (), s32[]{:S(2)}) async-start(), calls=%async_computation.9 | async-start | bytes 2621440 | tf_op jit(solution)/shard_map/all_gather | solution.py:162
  57.0 19.7 %copy-start.9 = (bf16[128,2048]{1,0:T(8,128)(2,1)S(1)}, bf16[128,2048]{1,0:T(8,128)(2,1)}, u32[]{:S(2)}) copy-start(bf16[128,2048]{1,0:T(8,128)(2,1)} %param.17) | copy-start | bytes 1572868
  74.6 154.1 %all-gather.10.cloned.1.call-start = ((), (), s32[]{:S(2)}) async-start(), calls=%async_computation.10 | async-start | bytes 9437184 | tf_op jit(solution)/shard_map/all_gather | solution.py:17
  75.0 18.6 %copy-start.4 = (bf16[128,2048]{0,1:T(8,128)(2,1)}, bf16[128,2048]{0,1:T(8,128)(2,1)S(1)}, u32[]{:S(2)}) copy-start(bf16[128,2048]{0,1:T(8,128)(2,1)S(1)} %copy.102) | copy-start | bytes 1572868
  95.2 17.7 %all-to-all-start.3 = ((bf16[32,8,1024]{2,0,1:T(8,128)(2,1)}), bf16[32,8,1024]{2,0,1:T(8,128)(2,1)S(1)}, u32[]{:S(2)}, u32[]{:S(2)}) async-start(bf16[32,8,1024]{2,0,1:T(8,128)(2,1)} %copy.89), calls=%async_computation.3 | async-start | bytes 1048576 | tf_op jit(solution)/shard_map/all_to_all | solution.py:154
  127.5 1.9 copy-start.1
  127.5 1.9 copy-start.3
  130.8 1.0 copy-start.2
  134.1 1.9 copy-start.1
  134.1 1.9 copy-start.3
  137.5 1.0 copy-start.2
  138.5 35.1 %copy-start.5 = (bf16[128,2048]{0,1:T(8,128)(2,1)S(1)}, bf16[128,2048]{0,1:T(8,128)(2,1)}, u32[]{:S(2)}) copy-start(bf16[128,2048]{0,1:T(8,128)(2,1)} %copy-done.4) | copy-start | bytes 1572868
  141.2 27.1 %all-to-all-start.6 = ((bf16[8,32,1024]{2,1,0:T(8,128)(2,1)}), bf16[8,32,1024]{2,1,0:T(8,128)(2,1)S(1)}, u32[]{:S(2)}, u32[]{:S(2)}) async-start(bf16[8,32,1024]{2,1,0:T(8,128)(2,1)} %convert_element_type.50), calls=%async_computation.6 | async-start | bytes 1048576 | tf_op jit(solution)/shard_map/all_to_all | solution.py:175
  170.0 12.3 %all-to-all-start.7 = ((bf16[32,4,2048]{2,0,1:T(8,128)(2,1)}), bf16[32,4,2048]{2,0,1:T(8,128)(2,1)S(1)}, u32[]{:S(2)}, u32[]{:S(2)}) async-start(bf16[32,4,2048]{2,0,1:T(8,128)(2,1)} %copy.97), calls=%async_computation.7 | async-start | bytes 1048576 | tf_op jit(solution)/shard_map/all_to_all | solution.py:174
  228.8 10.6 %copy-start.6 = (f32[128,16,128]{0,2,1:T(8,128)S(1)}, f32[128,16,128]{0,2,1:T(8,128)}, u32[]{:S(2)}) copy-start(f32[128,16,128]{0,2,1:T(8,128)} %convolution_bitcast_fusion.1) | copy-start | bytes 3145732
Sparse Core Ops, SparseCore 0:
  42.1 23.8 all-gather.5
  74.8 25.9 all-gather.7
  102.8 125.8 all-gather.9
where the time goes:
time: 250 us; the launch traced here: 249 us
  blocking collectives  106 us (42%)
  waiting for transfers between devices  66 us (26%)
  local copies, waits for them, and re-layouts  23.1 us (9%)
  other arithmetic  16.6 us (7%)
  between operations  14 us (6%)
  starting transfers between devices  10.7 us (4%)
  matrix products  9.5 us (4%)
  loops' own time  3.1 us (1%)
    all_gather x1, waiting for transfers between devices, entering(): pieces = jax.tree.map(lambda part: lax.all_gather(part, axis), value)  46.4 us
    all_gather x1, blocking collectives, entering(): pieces = jax.tree.map(lambda part: lax.all_gather(part, axis), value)  23.2 us
    all_to_all x1, blocking collectives, softmax_core(): lax.all_to_all(key_moved, 'ctx', split_axis=1, concat_axis=0, tiled=True)  20.6 us
    all_to_all x1, blocking collectives, softmax_core(): lax.all_to_all(value_moved, 'ctx', split_axis=1, concat_axis=0, tiled=True)  17.2 us
    all_to_all x1, blocking collectives, softmax_core(): lax.all_to_all(soft_query, 'head', split_axis=0, concat_axis=1, tiled=True)  16.9 us
    all_to_all x1, blocking collectives, softmax_core(): lax.all_to_all(soft_value, 'head', split_axis=0, concat_axis=1, tiled=True)  14.6 us
    all_to_all x1, waiting for transfers between devices, softmax_core(): lax.all_to_all(query_moved, 'ctx', split_axis=1, concat_axis=0, tiled=True)  13.5 us
    all_to_all x1, blocking collectives, softmax_core(): lax.all_to_all(soft_key, 'head', split_axis=0, concat_axis=1, tiled=True)  13.2 us
  transfers between devices with their start and end apart: 6, of which 4 were waited for; matrix products, arithmetic and copies ran while one was open for 13% of the time, Pallas kernels for 0%

commit v1 on v0

--- a/solution.py
+++ b/solution.py
@@ -1,9 +1,349 @@
+import functools
+
 import jax
 import jax.numpy as jnp
 from jax import lax
+from jax.experimental import pallas as pl
+from jax.experimental.pallas import tpu as pltpu
 from jax.sharding import PartitionSpec as P
 
 HEAD_DIM = 128
+NORM_EPS = 1e-06
+MASKED = -1e30
+F32 = jnp.float32
+BF16 = jnp.bfloat16
+
+
+def contract(a, b, dims):
+    return lax.dot_general(a, b, (dims, ((), ())), preferred_element_type=F32)
+
+
+def lanes(index):
+    return pl.ds(pl.multiple_of(index * HEAD_DIM, HEAD_DIM), HEAD_DIM)
+
+
+def kernel(
+    n,
+    lq, lk, lv, ld, sq, sk, sv,
+    lin_out, soft_out,
+    qs, ks, vs, qx, os, ox, os_in, ox_in, ls, lx, ls_in, lx_in,
+    st, st_in, ends, ends_in, pr, pr_in, tot, tot_in, rst, inside,
+    own_sem,
+    q_snd, q_rcv, k_snd, k_rcv, v_snd, v_rcv,
+    qx_snd, qx_rcv, st_snd, st_rcv, en_snd, en_rcv, tot_snd, tot_rcv,
+    pr_snd, pr_rcv, os_snd, os_rcv, ls_snd, ls_rcv, ox_snd, ox_rcv, lx_snd, lx_rcv,
+):
+    tokens = lq.shape[0]
+    heads = ld.shape[1]
+    half = n // 2
+    hp = heads // half
+    width = hp * HEAD_DIM
+    me = lax.axis_index("ctx")
+    side = me // half
+    r = lax.rem(me, half)
+    lower = side == 0
+    upper = side == 1
+
+    def peer(d):
+        return lax.rem(r + d, half)
+
+    def source(d):
+        return lax.rem(r + half - d, half)
+
+    def cols(index):
+        return pl.ds(pl.multiple_of(index * width, width), width)
+
+    def rows(index):
+        if isinstance(index, int):
+            return pl.ds(index * tokens, tokens)
+        return pl.ds(pl.multiple_of(index * tokens, tokens), tokens)
+
+    def remote(src, dst, snd, rcv, target):
+        return pltpu.make_async_remote_copy(
+            src_ref=src, dst_ref=dst, send_sem=snd, recv_sem=rcv,
+            device_id={"ctx": target}, device_id_type=pl.DeviceIdType.MESH,
+        )
+
+    def here(index):
+        return side * half + index
+
+    def q_copy(d):
+        j = peer(d)
+        return remote(sq.at[:, cols(j)], qs.at[rows(r), :], q_snd.at[d], q_rcv.at[d], here(j))
+
+    def k_copy(d):
+        j = peer(d)
+        return remote(sk.at[:, cols(j)], ks.at[rows(r), :], k_snd.at[d], k_rcv.at[d], here(j))
+
+    def v_copy(d):
+        j = peer(d)
+        return remote(sv.at[:, cols(j)], vs.at[rows(r), :], v_snd.at[d], v_rcv.at[d], here(j))
+
+    def qx_copy(i, d):
+        j = peer(d)
+        return remote(
+            sq.at[:, lanes(j * hp + i)], qx.at[rows(r), lanes(i)],
+            qx_snd.at[i, d], qx_rcv.at[i, d], j,
+        )
+
+    def st_copy(d):
+        j = peer(d)
+        return remote(
+            st.at[pl.ds(j * hp, hp)], st_in.at[r], st_snd.at[d], st_rcv.at[d], here(j)
+        )
+
+    def en_copy(d):
+        return remote(ends, ends_in.at[r], en_snd.at[d], en_rcv.at[d], here(peer(d)))
+
+    def tot_copy():
+        return remote(tot, tot_in, tot_snd, tot_rcv, half + r)
+
+    def pr_copy(d):
+        j = peer(d)
+        return remote(pr.at[j], pr_in.at[r], pr_snd.at[d], pr_rcv.at[d], here(j))
+
+    def os_copy(d):
+        j = peer(d)
+        return remote(
+            os.at[rows(j), :], os_in.at[:, cols(r)], os_snd.at[d], os_rcv.at[d], here(j)
+        )
+
+    def ls_copy(d):
+        j = peer(d)
+        return remote(ls.at[j], ls_in.at[r], ls_snd.at[d], ls_rcv.at[d], here(j))
+
+    def ox_copy(i, j):
+        return remote(
+            ox.at[rows(j), lanes(i)], ox_in.at[:, lanes(r * hp + i)],
+            ox_snd.at[i, j], ox_rcv.at[i, r], half + j,
+        )
+
+    def ox_arrival(i, j):
+        return remote(
+            ox.at[rows(j), lanes(i)], ox_in.at[:, lanes(j * hp + i)],
+            ox_snd.at[i, j], ox_rcv.at[i, j], r,
+        )
+
+    def lx_copy(j):
+        return remote(lx.at[j], lx_in.at[r], lx_snd.at[j], lx_rcv.at[r], half + j)
+
+    def lx_arrival(j):
+        return remote(lx.at[j], lx_in.at[j], lx_snd.at[j], lx_rcv.at[j], r)
+
+    others = range(1, half)
+
+    barrier = pltpu.get_barrier_semaphore()
+    for step in range(1, n):
+        pl.semaphore_signal(
+            barrier, inc=1, device_id={"ctx": lax.rem(me + step, n)},
+            device_id_type=pl.DeviceIdType.MESH,
+        )
+    own = [
+        pltpu.make_async_copy(sq.at[:, cols(r)], qs.at[rows(r), :], own_sem.at[0]),
+        pltpu.make_async_copy(sk.at[:, cols(r)], ks.at[rows(r), :], own_sem.at[1]),
+        pltpu.make_async_copy(sv.at[:, cols(r)], vs.at[rows(r), :], own_sem.at[2]),
+    ]
+    for copy in own:
+        copy.start()
+    pl.semaphore_wait(barrier, n - 1)
+
+    @pl.when(upper)
+    def _():
+        for i in range(hp):
+            for d in range(half):
+                qx_copy(i, d).start()
+
+    for make in (k_copy, v_copy, q_copy):
+        for d in others:
+            make(d).start()
+
+    at_row = lax.broadcasted_iota(jnp.int32, (tokens, tokens), 0)
+    at_col = lax.broadcasted_iota(jnp.int32, (tokens, tokens), 1)
+    causal = at_row >= at_col
+    padded = jnp.concatenate(
+        [ld[...], jnp.zeros((tokens, HEAD_DIM - heads), F32)], axis=1
+    )
+    running = jnp.dot(
+        causal.astype(F32), padded, precision=lax.Precision.HIGHEST, preferred_element_type=F32
+    )
+    rst[...] = running.T
+    ends[...] = jnp.broadcast_to(rst[pl.ds(0, heads), tokens - 1 :], ends.shape)
+
+    def states(h, carry):
+        down = jnp.broadcast_to(rst[pl.ds(h, 1), :], (tokens, tokens)).T
+        to_end = jnp.exp(down[tokens - 1 :, :] - down)
+        scaled = (lk[:, lanes(h)].astype(F32) * to_end).astype(BF16)
+        st[h] = contract(scaled, lv[:, lanes(h)], ((0,), (0,))).astype(BF16)
+        return carry
+
+    lax.fori_loop(0, heads, states, 0)
+    for d in others:
+        en_copy(d).start()
+        st_copy(d).start()
+
+    def within(h, carry):
+        across = jnp.broadcast_to(rst[pl.ds(h, 1), :], (tokens, tokens))
+        spread = jnp.where(causal, across.T - across, 0.0)
+        scores = contract(lq[:, lanes(h)], lk[:, lanes(h)], ((1,), (1,)))
+        decayed = jnp.where(causal, jnp.exp(spread) * scores, 0.0).astype(BF16)
+        inside[:, lanes(h)] = contract(decayed, lv[:, lanes(h)], ((1,), (0,)))
+        return carry
+
+    lax.fori_loop(0, heads, within, 0)
+
+    def attend(query, keys, values, block):
+        scores = contract(query, keys, ((1,), (1,))) * HEAD_DIM ** (-0.5)
+        if block is not None:
+            row = lax.broadcasted_iota(jnp.int32, scores.shape, 0) + block * tokens
+            col = lax.broadcasted_iota(jnp.int32, scores.shape, 1)
+            scores = jnp.where(col <= row, scores, MASKED)
+        peak = jnp.max(scores, axis=1, keepdims=True)
+        expo = jnp.exp(scores - peak)
+        mass = jnp.sum(expo, axis=1, keepdims=True)
+        result = contract(expo.astype(BF16), values, ((1,), (0,))) / mass
+        level = jnp.broadcast_to(peak + jnp.log(mass), (tokens, tokens)).T
+        return result.astype(BF16), level[0:1, :]
+
+    def crossing(i, carry):
+        for d in range(half):
+            qx_copy(i, d).wait_recv()
+        keys = ks[:, lanes(i)]
+        values = vs[:, lanes(i)]
+        for b in range(half):
+            result, level = attend(qx[rows(b), lanes(i)], keys, values, None)
+            ox[rows(b), lanes(i)] = result
+            lx[b, pl.ds(i, 1), :] = level
+            ox_copy(i, b).start()
+        return carry
+
+    def local(i, carry):
+        for b in range(half):
+            upto = (b + 1) * tokens
+            result, level = attend(
+                qs[rows(b), lanes(i)], ks[:upto, lanes(i)], vs[:upto, lanes(i)], b
+            )
+            os[rows(b), lanes(i)] = result
+            ls[b, pl.ds(i, 1), :] = level
+        return carry
+
+    def priors():
+        for d in others:
+            en_copy(d).wait_recv()
+            st_copy(d).wait_recv()
+
+        st_in[r] = st[pl.ds(r * hp, hp)]
+        ends_in[r] = ends[...]
+
+        def one(i, carry):
+            state = jnp.where(upper, tot_in[i].astype(F32), 0.0)
+            for c in range(half):
+                pr[c, i] = state.astype(BF16)
+                keep = jnp.exp(ends_in[c, pl.ds(r * hp + i, 1), :])
+                state = keep * state + st_in[c, i].astype(F32)
+            tot[i] = state.astype(BF16)
+            return carry
+
+        lax.fori_loop(0, hp, one, 0)
+
+    for d in others:
+        k_copy(d).wait_recv()
+        v_copy(d).wait_recv()
+    for copy in own:
+        copy.wait()
+
+    @pl.when(lower)
+    def _():
+        tot_in[...] = jnp.zeros_like(tot_in)
+        lax.fori_loop(0, (hp + 1) // 2, crossing, 0)
+        priors()
+        tot_copy().start()
+        lax.fori_loop((hp + 1) // 2, hp, crossing, 0)
+        for b in range(half):
+            lx_copy(b).start()
+
+    for d in others:
+        q_copy(d).wait_recv()
+    lax.fori_loop(0, hp, local, 0)
+    for d in others:
+        os_copy(d).start()
+        ls_copy(d).start()
+
+    @pl.when(upper)
+    def _():
+        tot_copy().wait_recv()
+        priors()
+
+    for d in others:
+        pr_copy(d).start()
+    pr_in[r] = pr[r]
+    os_in[:, cols(r)] = os[rows(r), :]
+    ls_in[r] = ls[r]
+
+    for d in others:
+        pr_copy(d).wait_recv()
+
+    def finish(j, carry):
+        def head(i, inner):
+            h = j * hp + i
+            down = jnp.broadcast_to(rst[pl.ds(h, 1), :], (tokens, tokens)).T
+            scaled = (lq[:, lanes(h)].astype(F32) * jnp.exp(down)).astype(BF16)
+            total = inside[:, lanes(h)] + contract(scaled, pr_in[j, i], ((1,), (0,)))
+            norm = lax.rsqrt(jnp.mean(total * total, axis=1, keepdims=True) + NORM_EPS)
+            lin_out[:, lanes(h)] = (total * norm).astype(BF16)
+            return inner
+
+        return lax.fori_loop(0, hp, head, carry)
+
+    lax.fori_loop(0, half, finish, 0)
+
+    for d in others:
+        os_copy(d).wait_recv()
+        ls_copy(d).wait_recv()
+
+    @pl.when(lower)
+    def _():
+        soft_out[...] = os_in[...]
+
+    @pl.when(upper)
+    def _():
+        for j in range(half):
+            lx_arrival(j).wait_recv()
+            for i in range(hp):
+                ox_arrival(i, j).wait_recv()
+
+        def merge(j, carry):
+            def head(i, inner):
+                h = j * hp + i
+                gap = lx_in[j, pl.ds(i, 1), :] - ls_in[j, pl.ds(i, 1), :]
+                gap = jnp.broadcast_to(gap, (tokens, tokens)).T
+                near = 1.0 / (1.0 + jnp.exp(gap))
+                far = 1.0 / (1.0 + jnp.exp(-gap))
+                mixed = near * os_in[:, lanes(h)].astype(F32)
+                mixed = mixed + far * ox_in[:, lanes(h)].astype(F32)
+                soft_out[:, lanes(h)] = mixed.astype(BF16)
+                return inner
+
+            return lax.fori_loop(0, hp, head, carry)
+
+        lax.fori_loop(0, half, merge, 0)
+
+    for make in (k_copy, v_copy, q_copy, en_copy, st_copy, pr_copy, os_copy, ls_copy):
+        for d in others:
+            make(d).wait_send()
+
+    @pl.when(upper)
+    def _():
+        for i in range(hp):
+            for d in range(half):
+                qx_copy(i, d).wait_send()
+
+    @pl.when(lower)
+    def _():
+        tot_copy().wait_send()
+        for j in range(half):
+            lx_copy(j).wait_send()
+            for i in range(hp):
+                ox_copy(i, j).wait_send()
 
 
 norm_eps = 1e-06
@@ -180,21 +520,70 @@
     )
 
 
-def shards(lin_query, lin_key, lin_value, log_decay, soft_query, soft_key, soft_value):
+def plain_shards(lin_query, lin_key, lin_value, log_decay, soft_query, soft_key, soft_value):
     lin_out = lightning_core(lin_query, lin_key, lin_value, log_decay)
     soft_out = softmax_core(soft_query, soft_key, soft_value)
     return (lin_out, soft_out)
 
 
+def shards(lin_query, lin_key, lin_value, log_decay, soft_query, soft_key, soft_value):
+    n = lax.axis_size("ctx")
+    tokens, columns = lin_query.shape
+    heads = log_decay.shape[1]
+    half = n // 2
+    hp = heads // half
+    width = hp * HEAD_DIM
+    level_rows = -(-hp // 8) * 8
+    vmem = pl.BlockSpec(memory_space=pltpu.VMEM)
+    far = pl.BlockSpec(memory_space=pl.ANY)
+    big = pltpu.VMEM((half * tokens, width), BF16)
+    full = pltpu.VMEM((tokens, columns), BF16)
+    level = pltpu.VMEM((half, level_rows, tokens), F32)
+    grid_states = pltpu.VMEM((half, hp, HEAD_DIM, HEAD_DIM), BF16)
+    some_states = pltpu.VMEM((hp, HEAD_DIM, HEAD_DIM), BF16)
+    dma = pltpu.SemaphoreType.DMA
+    ring = [dma((half,)), dma((half,))]
+    square = [dma((hp, half)), dma((hp, half))]
+    single = [dma, dma]
+    return pl.pallas_call(
+        functools.partial(kernel, n),
+        out_shape=[jax.ShapeDtypeStruct((tokens, columns), BF16)] * 2,
+        in_specs=[vmem] * 4 + [far] * 3,
+        out_specs=[vmem] * 2,
+        scratch_shapes=[big] * 6 + [full] * 2 + [level] * 4
+        + [
+            pltpu.VMEM((heads, HEAD_DIM, HEAD_DIM), BF16),
+            grid_states,
+            pltpu.VMEM((heads, tokens), F32),
+            pltpu.VMEM((half, heads, tokens), F32),
+            grid_states,
+            grid_states,
+            some_states,
+            some_states,
+            pltpu.VMEM((HEAD_DIM, tokens), F32),
+            pltpu.VMEM((tokens, columns), F32),
+            dma((3,)),
+        ]
+        + ring * 3 + square + ring * 2 + single + ring * 3 + square + ring,
+        compiler_params=pltpu.CompilerParams(
+            collective_id=0, has_side_effects=True, vmem_limit_bytes=40 * 1024 * 1024
+        ),
+        cost_estimate=pl.CostEstimate(
+            flops=3 * 10**9, bytes_accessed=4 * 10**6, transcendentals=3 * 10**6
+        ),
+    )(lin_query, lin_key, lin_value, log_decay, soft_query, soft_key, soft_value)
+
+
 def solution(mesh):
-    in_specs = (
-        P("ctx", "head"),
-        P("ctx", "head"),
-        P("ctx", "head"),
-        P("ctx", "head"),
-        P("ctx", "head"),
-        P("ctx", "head"),
-        P("ctx", "head"),
-    )
-    out_specs = (P("ctx", "head"), P("ctx", "head"))
-    return jax.shard_map(shards, mesh=mesh, in_specs=in_specs, out_specs=out_specs, check_vma=False)
+    spec = P("ctx", "head")
+    n = mesh.shape["ctx"]
+
+    def body(*args):
+        heads = args[3].shape[1]
+        if n % 2 or n < 4 or heads % (n // 2):
+            return plain_shards(*args)
+        return shards(*args)
+
+    return jax.shard_map(
+        body, mesh=mesh, in_specs=(spec,) * 7, out_specs=(spec,) * 2, check_vma=False
+    )

time: 250 us -> 76.8 us (0.31)
  the two profiles are of different devices: /device:TPU:0 before, /device:TPU:10 now
where the time goes in v1:
time: 76.8 us; the launch traced here: 76.3 us
  Pallas kernels  67.1 us (87%)
  local copies, waits for them, and re-layouts  8.63 us (11%)
    pallas_call x1, Pallas kernels, shards(): pl.pallas_call(functools.partial(kernel, n), out_shape=[jax.ShapeDtypeStr...  67.1 us
    unnamed x15, local copies, waits for them, and re-layouts  8.63 us

profile of v1, /device:TPU:10, one launch (start us, length us, event | category | flops | bytes accessed | tf_op | source)
XLA Modules:
  0.0 76.3 jit_solution(15019748282755767759)
XLA Ops:
  0.6 0.8 %copy.9.ld = f32[128,16]{1,0:T(8,128)S(1)} copy(f32[128,16]{0,1:T(8,128)} %param.10) | data formatting | bytes 16384 | tf_op args[3]
  1.4 0.0 copy-start
  1.4 1.0 %copy-done = bf16[128,2048]{1,0:T(8,128)(2,1)S(1)} copy-done((bf16[128,2048]{1,0:T(8,128)(2,1)S(1)}, bf16[128,2048]{1,0:T(8,128)(2,1)}, u32[]{:S(2)}) %copy-start) | copy-done | bytes 524312
  2.5 0.0 copy-start.1
  2.5 1.0 %copy-done.1 = bf16[128,2048]{1,0:T(8,128)(2,1)S(1)} copy-done((bf16[128,2048]{1,0:T(8,128)(2,1)S(1)}, bf16[128,2048]{1,0:T(8,128)(2,1)}, u32[]{:S(2)}) %copy-start.1) | copy-done | bytes 524312
  3.5 0.0 copy-start.2
  3.5 1.0 %copy-done.2 = bf16[128,2048]{1,0:T(8,128)(2,1)S(1)} copy-done((bf16[128,2048]{1,0:T(8,128)(2,1)S(1)}, bf16[128,2048]{1,0:T(8,128)(2,1)}, u32[]{:S(2)}) %copy-start.2) | copy-done | bytes 524312
  4.6 0.0 copy-start.3
  4.6 1.0 %copy-done.3 = bf16[128,2048]{1,0:T(8,128)(2,1)S(1)} copy-done((bf16[128,2048]{1,0:T(8,128)(2,1)S(1)}, bf16[128,2048]{1,0:T(8,128)(2,1)}, u32[]{:S(2)}) %copy-start.3) | copy-done | bytes 524312
  5.6 0.0 copy-start.4
  5.6 1.0 %copy-done.4 = bf16[128,2048]{1,0:T(8,128)(2,1)S(1)} copy-done((bf16[128,2048]{1,0:T(8,128)(2,1)S(1)}, bf16[128,2048]{1,0:T(8,128)(2,1)}, u32[]{:S(2)}) %copy-start.4) | copy-done | bytes 524312
  6.6 0.0 copy-start.5
  6.6 1.0 %copy-done.5 = bf16[128,2048]{1,0:T(8,128)(2,1)S(1)} copy-done((bf16[128,2048]{1,0:T(8,128)(2,1)S(1)}, bf16[128,2048]{1,0:T(8,128)(2,1)}, u32[]{:S(2)}) %copy-start.5) | copy-done | bytes 524312
  7.7 67.1 %shard_map.86 = (bf16[128,2048]{1,0:T(8,128)(2,1)S(1)}, bf16[128,2048]{1,0:T(8,128)(2,1)S(1)}) custom-call(bf16[128,2048]{1,0:T(8,128)(2,1)S(1)} %copy-done, bf16[128,2048]{1,0:T(8,128)(2,1)S(1)} %copy-done.1, bf16[128,2048]{1,0:T(8,128)(2,1)S(1)} %copy-done.2, f32[128,16]{1,0:T(8,128)S(1)} %copy.9.ld, bf16[128,2048]{1,0:T(8,128)(2,1)S(1)} %copy-done.3, ...), custom_call_target="tpu_custom_call" | custom-call | flops 3000000000 | bytes 4000000 | tf_op jit(solution)/shard_map/pallas_call | solution.py:548
  74.7 0.8 %copy.12 = bf16[128,2048]{1,0:T(8,128)(2,1)} copy(bf16[128,2048]{1,0:T(8,128)(2,1)S(1)} %get-tuple-element.4) | data formatting | bytes 1048576
  75.5 0.8 %copy.13 = bf16[128,2048]{1,0:T(8,128)(2,1)} copy(bf16[128,2048]{1,0:T(8,128)(2,1)S(1)} %get-tuple-element.5) | data formatting | bytes 1048576
Async XLA Ops:
  1.4 1.0 %copy-start = (bf16[128,2048]{1,0:T(8,128)(2,1)S(1)}, bf16[128,2048]{1,0:T(8,128)(2,1)}, u32[]{:S(2)}) copy-start(bf16[128,2048]{1,0:T(8,128)(2,1)} %lq.1) | copy-start | bytes 1572868
  2.5 1.0 %copy-start.1 = (bf16[128,2048]{1,0:T(8,128)(2,1)S(1)}, bf16[128,2048]{1,0:T(8,128)(2,1)}, u32[]{:S(2)}) copy-start(bf16[128,2048]{1,0:T(8,128)(2,1)} %lk.1) | copy-start | bytes 1572868
  3.5 1.0 %copy-start.2 = (bf16[128,2048]{1,0:T(8,128)(2,1)S(1)}, bf16[128,2048]{1,0:T(8,128)(2,1)}, u32[]{:S(2)}) copy-start(bf16[128,2048]{1,0:T(8,128)(2,1)} %lv.1) | copy-start | bytes 1572868
  4.6 1.0 %copy-start.3 = (bf16[128,2048]{1,0:T(8,128)(2,1)S(1)}, bf16[128,2048]{1,0:T(8,128)(2,1)}, u32[]{:S(2)}) copy-start(bf16[128,2048]{1,0:T(8,128)(2,1)} %sq.1) | copy-start | bytes 1572868
  5.6 1.0 %copy-start.4 = (bf16[128,2048]{1,0:T(8,128)(2,1)S(1)}, bf16[128,2048]{1,0:T(8,128)(2,1)}, u32[]{:S(2)}) copy-start(bf16[128,2048]{1,0:T(8,128)(2,1)} %sk.1) | copy-start | bytes 1572868
  6.6 1.0 %copy-start.5 = (bf16[128,2048]{1,0:T(8,128)(2,1)S(1)}, bf16[128,2048]{1,0:T(8,128)(2,1)}, u32[]{:S(2)}) copy-start(bf16[128,2048]{1,0:T(8,128)(2,1)} %sv.1) | copy-start | bytes 1572868

commit v2 on v1

--- a/solution.py
+++ b/solution.py
@@ -10,6 +10,7 @@
 HEAD_DIM = 128
 NORM_EPS = 1e-06
 MASKED = -1e30
+SCORE_SCALE = HEAD_DIM ** (-0.5) * 1.4426950408889634
 F32 = jnp.float32
 BF16 = jnp.bfloat16
 
@@ -24,9 +25,9 @@
 
 def kernel(
     n,
-    lq, lk, lv, ld, sq, sk, sv,
+    lq_far, lk_far, lv_far, ld, sq, sk, sv,
     lin_out, soft_out,
-    qs, ks, vs, qx, os, ox, os_in, ox_in, ls, lx, ls_in, lx_in,
+    lq, lk, lv, qs, ks, vs, qx, os, ox, os_in, ox_in, ls, lx, ls_in, lx_in,
     st, st_in, ends, ends_in, pr, pr_in, tot, tot_in, rst, inside,
     own_sem,
     q_snd, q_rcv, k_snd, k_rcv, v_snd, v_rcv,
@@ -34,7 +35,7 @@
     pr_snd, pr_rcv, os_snd, os_rcv, ls_snd, ls_rcv, ox_snd, ox_rcv, lx_snd, lx_rcv,
 ):
     tokens = lq.shape[0]
-    heads = ld.shape[1]
+    heads = ld.shape[0]
     half = n // 2
     hp = heads // half
     width = hp * HEAD_DIM
@@ -139,6 +140,9 @@
             device_id_type=pl.DeviceIdType.MESH,
         )
     own = [
+        pltpu.make_async_copy(lk_far, lk, own_sem.at[3]),
+        pltpu.make_async_copy(lv_far, lv, own_sem.at[4]),
+        pltpu.make_async_copy(lq_far, lq, own_sem.at[5]),
         pltpu.make_async_copy(sq.at[:, cols(r)], qs.at[rows(r), :], own_sem.at[0]),
         pltpu.make_async_copy(sk.at[:, cols(r)], ks.at[rows(r), :], own_sem.at[1]),
         pltpu.make_async_copy(sv.at[:, cols(r)], vs.at[rows(r), :], own_sem.at[2]),
@@ -160,14 +164,13 @@
     at_row = lax.broadcasted_iota(jnp.int32, (tokens, tokens), 0)
     at_col = lax.broadcasted_iota(jnp.int32, (tokens, tokens), 1)
     causal = at_row >= at_col
-    padded = jnp.concatenate(
-        [ld[...], jnp.zeros((tokens, HEAD_DIM - heads), F32)], axis=1
-    )
-    running = jnp.dot(
-        causal.astype(F32), padded, precision=lax.Precision.HIGHEST, preferred_element_type=F32
-    )
-    rst[...] = running.T
-    ends[...] = jnp.broadcast_to(rst[pl.ds(0, heads), tokens - 1 :], ends.shape)
+    rst[...] = jnp.dot(
+        ld[...], (at_row <= at_col).astype(F32),
+        precision=lax.Precision.HIGHEST, preferred_element_type=F32,
+    )
+    for copy in own[:3]:
+        copy.wait()
+    ends[...] = jnp.broadcast_to(rst[:, tokens - 1 :], ends.shape)
 
     def states(h, carry):
         down = jnp.broadcast_to(rst[pl.ds(h, 1), :], (tokens, tokens)).T
@@ -176,7 +179,7 @@
         st[h] = contract(scaled, lv[:, lanes(h)], ((0,), (0,))).astype(BF16)
         return carry
 
-    lax.fori_loop(0, heads, states, 0)
+    lax.fori_loop(0, heads, states, 0, unroll=4)
     for d in others:
         en_copy(d).start()
         st_copy(d).start()
@@ -189,19 +192,19 @@
         inside[:, lanes(h)] = contract(decayed, lv[:, lanes(h)], ((1,), (0,)))
         return carry
 
-    lax.fori_loop(0, heads, within, 0)
+    lax.fori_loop(0, heads, within, 0, unroll=4)
 
     def attend(query, keys, values, block):
-        scores = contract(query, keys, ((1,), (1,))) * HEAD_DIM ** (-0.5)
+        scores = contract(query, keys, ((1,), (1,)))
         if block is not None:
             row = lax.broadcasted_iota(jnp.int32, scores.shape, 0) + block * tokens
             col = lax.broadcasted_iota(jnp.int32, scores.shape, 1)
             scores = jnp.where(col <= row, scores, MASKED)
-        peak = jnp.max(scores, axis=1, keepdims=True)
-        expo = jnp.exp(scores - peak)
+        peak = jnp.max(scores, axis=1, keepdims=True) * SCORE_SCALE
+        expo = jnp.exp2(scores * SCORE_SCALE - peak)
         mass = jnp.sum(expo, axis=1, keepdims=True)
-        result = contract(expo.astype(BF16), values, ((1,), (0,))) / mass
-        level = jnp.broadcast_to(peak + jnp.log(mass), (tokens, tokens)).T
+        result = contract(expo.astype(BF16), values, ((1,), (0,))) * (1.0 / mass)
+        level = jnp.broadcast_to(peak + jnp.log2(mass), (tokens, tokens)).T
         return result.astype(BF16), level[0:1, :]
 
     def crossing(i, carry):
@@ -213,6 +216,7 @@
             result, level = attend(qx[rows(b), lanes(i)], keys, values, None)
             ox[rows(b), lanes(i)] = result
             lx[b, pl.ds(i, 1), :] = level
+        for b in range(half):
             ox_copy(i, b).start()
         return carry
 
@@ -243,12 +247,12 @@
             tot[i] = state.astype(BF16)
             return carry
 
-        lax.fori_loop(0, hp, one, 0)
+        lax.fori_loop(0, hp, one, 0, unroll=2)
 
     for d in others:
         k_copy(d).wait_recv()
         v_copy(d).wait_recv()
-    for copy in own:
+    for copy in own[3:]:
         copy.wait()
 
     @pl.when(lower)
@@ -292,7 +296,7 @@
             lin_out[:, lanes(h)] = (total * norm).astype(BF16)
             return inner
 
-        return lax.fori_loop(0, hp, head, carry)
+        return lax.fori_loop(0, hp, head, carry, unroll=True)
 
     lax.fori_loop(0, half, finish, 0)
 
@@ -316,14 +320,14 @@
                 h = j * hp + i
                 gap = lx_in[j, pl.ds(i, 1), :] - ls_in[j, pl.ds(i, 1), :]
                 gap = jnp.broadcast_to(gap, (tokens, tokens)).T
-                near = 1.0 / (1.0 + jnp.exp(gap))
-                far = 1.0 / (1.0 + jnp.exp(-gap))
+                near = 1.0 / (1.0 + jnp.exp2(gap))
+                far = 1.0 / (1.0 + jnp.exp2(-gap))
                 mixed = near * os_in[:, lanes(h)].astype(F32)
                 mixed = mixed + far * ox_in[:, lanes(h)].astype(F32)
                 soft_out[:, lanes(h)] = mixed.astype(BF16)
                 return inner
 
-            return lax.fori_loop(0, hp, head, carry)
+            return lax.fori_loop(0, hp, head, carry, unroll=True)
 
         lax.fori_loop(0, half, merge, 0)
 
@@ -535,7 +539,7 @@
     width = hp * HEAD_DIM
     level_rows = -(-hp // 8) * 8
     vmem = pl.BlockSpec(memory_space=pltpu.VMEM)
-    far = pl.BlockSpec(memory_space=pl.ANY)
+    far = pl.BlockSpec(memory_space=pltpu.HBM)
     big = pltpu.VMEM((half * tokens, width), BF16)
     full = pltpu.VMEM((tokens, columns), BF16)
     level = pltpu.VMEM((half, level_rows, tokens), F32)
@@ -548,9 +552,9 @@
     return pl.pallas_call(
         functools.partial(kernel, n),
         out_shape=[jax.ShapeDtypeStruct((tokens, columns), BF16)] * 2,
-        in_specs=[vmem] * 4 + [far] * 3,
+        in_specs=[far] * 3 + [vmem] + [far] * 3,
         out_specs=[vmem] * 2,
-        scratch_shapes=[big] * 6 + [full] * 2 + [level] * 4
+        scratch_shapes=[full] * 3 + [big] * 6 + [full] * 2 + [level] * 4
         + [
             pltpu.VMEM((heads, HEAD_DIM, HEAD_DIM), BF16),
             grid_states,
@@ -560,18 +564,18 @@
             grid_states,
             some_states,
             some_states,
-            pltpu.VMEM((HEAD_DIM, tokens), F32),
+            pltpu.VMEM((heads, tokens), F32),
             pltpu.VMEM((tokens, columns), F32),
-            dma((3,)),
+            dma((6,)),
         ]
         + ring * 3 + square + ring * 2 + single + ring * 3 + square + ring,
         compiler_params=pltpu.CompilerParams(
-            collective_id=0, has_side_effects=True, vmem_limit_bytes=40 * 1024 * 1024
+            collective_id=0, has_side_effects=True, vmem_limit_bytes=60 * 1024 * 1024
         ),
         cost_estimate=pl.CostEstimate(
             flops=3 * 10**9, bytes_accessed=4 * 10**6, transcendentals=3 * 10**6
         ),
-    )(lin_query, lin_key, lin_value, log_decay, soft_query, soft_key, soft_value)
+    )(lin_query, lin_key, lin_value, log_decay.T, soft_query, soft_key, soft_value)
 
 
 def solution(mesh):

time: 76.8 us -> 69 us (0.90)
  local copies, waits for them, and re-layouts: 8.63 us -> 2.74 us
  Pallas kernels: 67.1 us -> 65.4 us
    unnamed x15 -> x4, local copies, waits for them, and re-layouts: 8.63 us -> 2.74 us
    pallas_call x1, Pallas kernels: 67.1 us -> 65.4 us  [shards(): pl.pallas_call(functools.partial(kernel, n), out_shape=[jax.ShapeDtypeStr...]
where the time goes in v2:
time: 69 us; the launch traced here: 68.7 us
  Pallas kernels  65.4 us (95%)
  local copies, waits for them, and re-layouts  2.74 us (4%)
    pallas_call x1, Pallas kernels, shards(): pl.pallas_call(functools.partial(kernel, n), out_shape=[jax.ShapeDtypeStr...  65.4 us
    unnamed x4, local copies, waits for them, and re-layouts  2.74 us

profile of v2, /device:TPU:10, one launch (start us, length us, event | category | flops | bytes accessed | tf_op | source)
XLA Modules:
  0.0 68.7 jit_solution(16214724325516184516)
XLA Ops:
  0.6 65.4 %shard_map.86 = (bf16[128,2048]{1,0:T(8,128)(2,1)}, bf16[128,2048]{1,0:T(8,128)(2,1)}) custom-call(bf16[128,2048]{1,0:T(8,128)(2,1)} %lq_far.1, bf16[128,2048]{1,0:T(8,128)(2,1)} %lk_far.1, bf16[128,2048]{1,0:T(8,128)(2,1)} %lv_far.1, f32[16,128]{1,0:T(8,128)} %bitcast.1, bf16[128,2048]{1,0:T(8,128)(2,1)} %sq.1, bf16[128,2048]{1,0:T(8,128)(2,1)} %sk.1, ...), custom_call_target="tpu_custom_call" | custom-call | flops 3000000000 | bytes 4000000 | tf_op jit(solution)/shard_map/pallas_call | solution.py:552
  66.0 0.0 copy-start
  66.0 1.9 %copy.11 = bf16[128,2048]{1,0:T(8,128)(2,1)} copy(bf16[128,2048]{1,0:T(8,128)(2,1)} %get-tuple-element.4) | data formatting | bytes 1048576
  68.0 0.0 copy-done
  68.0 0.8 %copy.12 = bf16[128,2048]{1,0:T(8,128)(2,1)} copy(bf16[128,2048]{1,0:T(8,128)(2,1)S(1)} %copy-done) | data formatting | bytes 1048576
Async XLA Ops:
  66.0 2.0 %copy-start = (bf16[128,2048]{1,0:T(8,128)(2,1)S(1)}, bf16[128,2048]{1,0:T(8,128)(2,1)}, u32[]{:S(2)}) copy-start(bf16[128,2048]{1,0:T(8,128)(2,1)} %get-tuple-element.5) | copy-start | bytes 1572868

commit v3 on v2

--- a/solution.py
+++ b/solution.py
@@ -68,17 +68,26 @@
     def here(index):
         return side * half + index
 
-    def q_copy(d):
-        j = peer(d)
-        return remote(sq.at[:, cols(j)], qs.at[rows(r), :], q_snd.at[d], q_rcv.at[d], here(j))
-
-    def k_copy(d):
-        j = peer(d)
-        return remote(sk.at[:, cols(j)], ks.at[rows(r), :], k_snd.at[d], k_rcv.at[d], here(j))
-
-    def v_copy(d):
-        j = peer(d)
-        return remote(sv.at[:, cols(j)], vs.at[rows(r), :], v_snd.at[d], v_rcv.at[d], here(j))
+    def q_copy(i, d):
+        j = peer(d)
+        return remote(
+            sq.at[:, lanes(j * hp + i)], qs.at[rows(r), lanes(i)],
+            q_snd.at[i, d], q_rcv.at[i, d], here(j),
+        )
+
+    def k_copy(i, d):
+        j = peer(d)
+        return remote(
+            sk.at[:, lanes(j * hp + i)], ks.at[rows(r), lanes(i)],
+            k_snd.at[i, d], k_rcv.at[i, d], here(j),
+        )
+
+    def v_copy(i, d):
+        j = peer(d)
+        return remote(
+            sv.at[:, lanes(j * hp + i)], vs.at[rows(r), lanes(i)],
+            v_snd.at[i, d], v_rcv.at[i, d], here(j),
+        )
 
     def qx_copy(i, d):
         j = peer(d)
@@ -103,10 +112,18 @@
         j = peer(d)
         return remote(pr.at[j], pr_in.at[r], pr_snd.at[d], pr_rcv.at[d], here(j))
 
-    def os_copy(d):
-        j = peer(d)
-        return remote(
-            os.at[rows(j), :], os_in.at[:, cols(r)], os_snd.at[d], os_rcv.at[d], here(j)
+    def os_copy(i, d):
+        j = peer(d)
+        return remote(
+            os.at[rows(j), lanes(i)], os_in.at[:, lanes(r * hp + i)],
+            os_snd.at[i, d], os_rcv.at[i, d], here(j),
+        )
+
+    def os_arrival(i, d):
+        j = source(d)
+        return remote(
+            os.at[rows(j), lanes(i)], os_in.at[:, lanes(j * hp + i)],
+            os_snd.at[i, d], os_rcv.at[i, d], here(j),
         )
 
     def ls_copy(d):
@@ -151,15 +168,22 @@
         copy.start()
     pl.semaphore_wait(barrier, n - 1)
 
-    @pl.when(upper)
-    def _():
-        for i in range(hp):
+    def spread_head(i, carry):
+        for make in (k_copy, v_copy):
+            for d in others:
+                make(i, d).start()
+
+        @pl.when(upper)
+        def _():
             for d in range(half):
                 qx_copy(i, d).start()
 
-    for make in (k_copy, v_copy, q_copy):
-        for d in others:
-            make(d).start()
+        for d in others:
+            q_copy(i, d).start()
+        return carry
+
+    first = (hp + 1) // 2
+    lax.fori_loop(0, first, spread_head, 0)
 
     at_row = lax.broadcasted_iota(jnp.int32, (tokens, tokens), 0)
     at_col = lax.broadcasted_iota(jnp.int32, (tokens, tokens), 1)
@@ -183,6 +207,7 @@
     for d in others:
         en_copy(d).start()
         st_copy(d).start()
+    lax.fori_loop(first, hp, spread_head, 0)
 
     def within(h, carry):
         across = jnp.broadcast_to(rst[pl.ds(h, 1), :], (tokens, tokens))
@@ -192,7 +217,6 @@
         inside[:, lanes(h)] = contract(decayed, lv[:, lanes(h)], ((1,), (0,)))
         return carry
 
-    lax.fori_loop(0, heads, within, 0, unroll=4)
 
     def attend(query, keys, values, block):
         scores = contract(query, keys, ((1,), (1,)))
@@ -207,20 +231,26 @@
         level = jnp.broadcast_to(peak + jnp.log2(mass), (tokens, tokens)).T
         return result.astype(BF16), level[0:1, :]
 
-    def crossing(i, carry):
-        for d in range(half):
-            qx_copy(i, d).wait_recv()
-        keys = ks[:, lanes(i)]
-        values = vs[:, lanes(i)]
-        for b in range(half):
-            result, level = attend(qx[rows(b), lanes(i)], keys, values, None)
-            ox[rows(b), lanes(i)] = result
-            lx[b, pl.ds(i, 1), :] = level
-        for b in range(half):
-            ox_copy(i, b).start()
-        return carry
-
-    def local(i, carry):
+    def head_step(i, carry):
+        for d in others:
+            k_copy(i, d).wait_recv()
+            v_copy(i, d).wait_recv()
+
+        @pl.when(lower)
+        def _():
+            for d in range(half):
+                qx_copy(i, d).wait_recv()
+            for b in range(half):
+                result, level = attend(
+                    qx[rows(b), lanes(i)], ks[:, lanes(i)], vs[:, lanes(i)], None
+                )
+                ox[rows(b), lanes(i)] = result
+                lx[b, pl.ds(i, 1), :] = level
+            for b in range(half):
+                ox_copy(i, b).start()
+
+        for d in others:
+            q_copy(i, d).wait_recv()
         for b in range(half):
             upto = (b + 1) * tokens
             result, level = attend(
@@ -228,6 +258,8 @@
             )
             os[rows(b), lanes(i)] = result
             ls[b, pl.ds(i, 1), :] = level
+        for d in others:
+            os_copy(i, d).start()
         return carry
 
     def priors():
@@ -249,36 +281,37 @@
 
         lax.fori_loop(0, hp, one, 0, unroll=2)
 
-    for d in others:
-        k_copy(d).wait_recv()
-        v_copy(d).wait_recv()
     for copy in own[3:]:
         copy.wait()
+
+    lax.fori_loop(0, first, head_step, 0)
 
     @pl.when(lower)
     def _():
         tot_in[...] = jnp.zeros_like(tot_in)
-        lax.fori_loop(0, (hp + 1) // 2, crossing, 0)
         priors()
         tot_copy().start()
-        lax.fori_loop((hp + 1) // 2, hp, crossing, 0)
+        for d in others:
+            pr_copy(d).start()
+
+    lax.fori_loop(first, hp, head_step, 0)
+
+    @pl.when(lower)
+    def _():
         for b in range(half):
             lx_copy(b).start()
 
     for d in others:
-        q_copy(d).wait_recv()
-    lax.fori_loop(0, hp, local, 0)
-    for d in others:
-        os_copy(d).start()
         ls_copy(d).start()
 
     @pl.when(upper)
     def _():
         tot_copy().wait_recv()
         priors()
-
-    for d in others:
-        pr_copy(d).start()
+        for d in others:
+            pr_copy(d).start()
+
+    lax.fori_loop(0, heads, within, 0, unroll=4)
     pr_in[r] = pr[r]
     os_in[:, cols(r)] = os[rows(r), :]
     ls_in[r] = ls[r]
@@ -301,7 +334,8 @@
     lax.fori_loop(0, half, finish, 0)
 
     for d in others:
-        os_copy(d).wait_recv()
+        for i in range(hp):
+            os_arrival(i, d).wait_recv()
         ls_copy(d).wait_recv()
 
     @pl.when(lower)
@@ -331,9 +365,13 @@
 
         lax.fori_loop(0, half, merge, 0)
 
-    for make in (k_copy, v_copy, q_copy, en_copy, st_copy, pr_copy, os_copy, ls_copy):
+    for make in (en_copy, st_copy, pr_copy, ls_copy):
         for d in others:
             make(d).wait_send()
+    for make in (k_copy, v_copy, q_copy, os_copy):
+        for i in range(hp):
+            for d in others:
+                make(i, d).wait_send()
 
     @pl.when(upper)
     def _():
@@ -568,7 +606,7 @@
             pltpu.VMEM((tokens, columns), F32),
             dma((6,)),
         ]
-        + ring * 3 + square + ring * 2 + single + ring * 3 + square + ring,
+        + square * 4 + ring * 2 + single + ring + square + ring + square + ring,
         compiler_params=pltpu.CompilerParams(
             collective_id=0, has_side_effects=True, vmem_limit_bytes=60 * 1024 * 1024
         ),

time: 69 us -> 62.4 us (0.904)
  Pallas kernels: 65.4 us -> 58.2 us
    pallas_call x1, Pallas kernels: 65.4 us -> 58.2 us  [shards(): pl.pallas_call(functools.partial(kernel, n), out_shape=[jax.ShapeDtypeStr...]
where the time goes in v3:
time: 62.4 us; the launch traced here: 61.6 us
  Pallas kernels  58.2 us (93%)
  local copies, waits for them, and re-layouts  2.74 us (4%)
  between operations  0.65 us (1%)
    pallas_call x1, Pallas kernels, shards(): pl.pallas_call(functools.partial(kernel, n), out_shape=[jax.ShapeDtypeStr...  58.2 us
    unnamed x4, local copies, waits for them, and re-layouts  2.74 us

profile of v3, /device:TPU:10, one launch (start us, length us, event | category | flops | bytes accessed | tf_op | source)
XLA Modules:
  0.0 61.6 jit_solution(95152349712462256)
XLA Ops:
  0.6 58.2 %shard_map.86 = (bf16[128,2048]{1,0:T(8,128)(2,1)}, bf16[128,2048]{1,0:T(8,128)(2,1)}) custom-call(bf16[128,2048]{1,0:T(8,128)(2,1)} %lq_far.1, bf16[128,2048]{1,0:T(8,128)(2,1)} %lk_far.1, bf16[128,2048]{1,0:T(8,128)(2,1)} %lv_far.1, f32[16,128]{1,0:T(8,128)} %bitcast.1, bf16[128,2048]{1,0:T(8,128)(2,1)} %sq.1, bf16[128,2048]{1,0:T(8,128)(2,1)} %sk.1, ...), custom_call_target="tpu_custom_call" | custom-call | flops 3000000000 | bytes 4000000 | tf_op jit(solution)/shard_map/pallas_call | solution.py:590
  58.8 0.0 copy-start
  58.9 1.9 %copy.11 = bf16[128,2048]{1,0:T(8,128)(2,1)} copy(bf16[128,2048]{1,0:T(8,128)(2,1)} %get-tuple-element.4) | data formatting | bytes 1048576
  60.8 0.0 copy-done
  60.8 0.8 %copy.12 = bf16[128,2048]{1,0:T(8,128)(2,1)} copy(bf16[128,2048]{1,0:T(8,128)(2,1)S(1)} %copy-done) | data formatting | bytes 1048576
Async XLA Ops:
  58.8 2.0 %copy-start = (bf16[128,2048]{1,0:T(8,128)(2,1)S(1)}, bf16[128,2048]{1,0:T(8,128)(2,1)}, u32[]{:S(2)}) copy-start(bf16[128,2048]{1,0:T(8,128)(2,1)} %get-tuple-element.5) | copy-start | bytes 1572868

commit v4 on v3

--- a/solution.py
+++ b/solution.py
@@ -26,7 +26,7 @@
 def kernel(
     n,
     lq_far, lk_far, lv_far, ld, sq, sk, sv,
-    lin_out, soft_out,
+    both_out,
     lq, lk, lv, qs, ks, vs, qx, os, ox, os_in, ox_in, ls, lx, ls_in, lx_in,
     st, st_in, ends, ends_in, pr, pr_in, tot, tot_in, rst, inside,
     own_sem,
@@ -36,9 +36,9 @@
 ):
     tokens = lq.shape[0]
     heads = ld.shape[0]
+    lin_out, soft_out = both_out.at[0], both_out.at[1]
     half = n // 2
     hp = heads // half
-    width = hp * HEAD_DIM
     me = lax.axis_index("ctx")
     side = me // half
     r = lax.rem(me, half)
@@ -51,9 +51,6 @@
     def source(d):
         return lax.rem(r + half - d, half)
 
-    def cols(index):
-        return pl.ds(pl.multiple_of(index * width, width), width)
-
     def rows(index):
         if isinstance(index, int):
             return pl.ds(index * tokens, tokens)
@@ -71,28 +68,28 @@
     def q_copy(i, d):
         j = peer(d)
         return remote(
-            sq.at[:, lanes(j * hp + i)], qs.at[rows(r), lanes(i)],
+            sq.at[:, lanes(j * hp + i)], qs.at[i, rows(r)],
             q_snd.at[i, d], q_rcv.at[i, d], here(j),
         )
 
     def k_copy(i, d):
         j = peer(d)
         return remote(
-            sk.at[:, lanes(j * hp + i)], ks.at[rows(r), lanes(i)],
+            sk.at[:, lanes(j * hp + i)], ks.at[i, rows(r)],
             k_snd.at[i, d], k_rcv.at[i, d], here(j),
         )
 
     def v_copy(i, d):
         j = peer(d)
         return remote(
-            sv.at[:, lanes(j * hp + i)], vs.at[rows(r), lanes(i)],
+            sv.at[:, lanes(j * hp + i)], vs.at[i, rows(r)],
             v_snd.at[i, d], v_rcv.at[i, d], here(j),
         )
 
     def qx_copy(i, d):
         j = peer(d)
         return remote(
-            sq.at[:, lanes(j * hp + i)], qx.at[rows(r), lanes(i)],
+            sq.at[:, lanes(j * hp + i)], qx.at[i, rows(r)],
             qx_snd.at[i, d], qx_rcv.at[i, d], j,
         )
 
@@ -115,38 +112,50 @@
     def os_copy(i, d):
         j = peer(d)
         return remote(
-            os.at[rows(j), lanes(i)], os_in.at[:, lanes(r * hp + i)],
+            os.at[i, rows(j)], os_in.at[r * hp + i],
             os_snd.at[i, d], os_rcv.at[i, d], here(j),
         )
 
     def os_arrival(i, d):
         j = source(d)
         return remote(
-            os.at[rows(j), lanes(i)], os_in.at[:, lanes(j * hp + i)],
+            os.at[i, rows(j)], os_in.at[j * hp + i],
             os_snd.at[i, d], os_rcv.at[i, d], here(j),
         )
 
-    def ls_copy(d):
-        j = peer(d)
-        return remote(ls.at[j], ls_in.at[r], ls_snd.at[d], ls_rcv.at[d], here(j))
+    def ls_copy(i, d):
+        j = peer(d)
+        return remote(
+            ls.at[j, i], ls_in.at[r, i], ls_snd.at[i, d], ls_rcv.at[i, d], here(j)
+        )
+
+    def ls_arrival(i, d):
+        j = source(d)
+        return remote(
+            ls.at[j, i], ls_in.at[j, i], ls_snd.at[i, d], ls_rcv.at[i, d], here(j)
+        )
 
     def ox_copy(i, j):
         return remote(
-            ox.at[rows(j), lanes(i)], ox_in.at[:, lanes(r * hp + i)],
+            ox.at[i, rows(j)], ox_in.at[r * hp + i],
             ox_snd.at[i, j], ox_rcv.at[i, r], half + j,
         )
 
     def ox_arrival(i, j):
         return remote(
-            ox.at[rows(j), lanes(i)], ox_in.at[:, lanes(j * hp + i)],
+            ox.at[i, rows(j)], ox_in.at[j * hp + i],
             ox_snd.at[i, j], ox_rcv.at[i, j], r,
         )
 
-    def lx_copy(j):
-        return remote(lx.at[j], lx_in.at[r], lx_snd.at[j], lx_rcv.at[r], half + j)
-
-    def lx_arrival(j):
-        return remote(lx.at[j], lx_in.at[j], lx_snd.at[j], lx_rcv.at[j], r)
+    def lx_copy(i, j):
+        return remote(
+            lx.at[j, i], lx_in.at[r, i], lx_snd.at[i, j], lx_rcv.at[i, r], half + j
+        )
+
+    def lx_arrival(i, j):
+        return remote(
+            lx.at[j, i], lx_in.at[j, i], lx_snd.at[i, j], lx_rcv.at[i, j], r
+        )
 
     others = range(1, half)
 
@@ -157,12 +166,16 @@
             device_id_type=pl.DeviceIdType.MESH,
         )
     own = [
-        pltpu.make_async_copy(lk_far, lk, own_sem.at[3]),
-        pltpu.make_async_copy(lv_far, lv, own_sem.at[4]),
-        pltpu.make_async_copy(lq_far, lq, own_sem.at[5]),
-        pltpu.make_async_copy(sq.at[:, cols(r)], qs.at[rows(r), :], own_sem.at[0]),
-        pltpu.make_async_copy(sk.at[:, cols(r)], ks.at[rows(r), :], own_sem.at[1]),
-        pltpu.make_async_copy(sv.at[:, cols(r)], vs.at[rows(r), :], own_sem.at[2]),
+        pltpu.make_async_copy(lk_far, lk, own_sem.at[0]),
+        pltpu.make_async_copy(lv_far, lv, own_sem.at[1]),
+        pltpu.make_async_copy(lq_far, lq, own_sem.at[2]),
+    ]
+    own += [
+        pltpu.make_async_copy(
+            whole.at[:, lanes(r * hp + i)], kept.at[i, rows(r)], own_sem.at[3 + a * hp + i]
+        )
+        for a, (whole, kept) in enumerate(((sq, qs), (sk, ks), (sv, vs)))
+        for i in range(hp)
     ]
     for copy in own:
         copy.start()
@@ -229,7 +242,7 @@
         mass = jnp.sum(expo, axis=1, keepdims=True)
         result = contract(expo.astype(BF16), values, ((1,), (0,))) * (1.0 / mass)
         level = jnp.broadcast_to(peak + jnp.log2(mass), (tokens, tokens)).T
-        return result.astype(BF16), level[0:1, :]
+        return result.astype(BF16), level[0:8, :]
 
     def head_step(i, carry):
         for d in others:
@@ -242,24 +255,26 @@
                 qx_copy(i, d).wait_recv()
             for b in range(half):
                 result, level = attend(
-                    qx[rows(b), lanes(i)], ks[:, lanes(i)], vs[:, lanes(i)], None
+                    qx[i, rows(b)], ks[i], vs[i], None
                 )
-                ox[rows(b), lanes(i)] = result
-                lx[b, pl.ds(i, 1), :] = level
+                ox[i, rows(b)] = result
+                lx[b, i] = level
             for b in range(half):
                 ox_copy(i, b).start()
+                lx_copy(i, b).start()
 
         for d in others:
             q_copy(i, d).wait_recv()
         for b in range(half):
             upto = (b + 1) * tokens
             result, level = attend(
-                qs[rows(b), lanes(i)], ks[:upto, lanes(i)], vs[:upto, lanes(i)], b
+                qs[i, rows(b)], ks[i, :upto], vs[i, :upto], b
             )
-            os[rows(b), lanes(i)] = result
-            ls[b, pl.ds(i, 1), :] = level
+            os[i, rows(b)] = result
+            ls[b, i] = level
         for d in others:
             os_copy(i, d).start()
+            ls_copy(i, d).start()
         return carry
 
     def priors():
@@ -296,14 +311,6 @@
 
     lax.fori_loop(first, hp, head_step, 0)
 
-    @pl.when(lower)
-    def _():
-        for b in range(half):
-            lx_copy(b).start()
-
-    for d in others:
-        ls_copy(d).start()
-
     @pl.when(upper)
     def _():
         tot_copy().wait_recv()
@@ -313,7 +320,7 @@
 
     lax.fori_loop(0, heads, within, 0, unroll=4)
     pr_in[r] = pr[r]
-    os_in[:, cols(r)] = os[rows(r), :]
+    os_in[pl.ds(r * hp, hp)] = os[:, rows(r), :]
     ls_in[r] = ls[r]
 
     for d in others:
@@ -333,42 +340,38 @@
 
     lax.fori_loop(0, half, finish, 0)
 
-    for d in others:
-        for i in range(hp):
+    def arrive(i, carry):
+        for d in others:
             os_arrival(i, d).wait_recv()
-        ls_copy(d).wait_recv()
-
-    @pl.when(lower)
-    def _():
-        soft_out[...] = os_in[...]
-
-    @pl.when(upper)
-    def _():
-        for j in range(half):
-            lx_arrival(j).wait_recv()
-            for i in range(hp):
+            ls_arrival(i, d).wait_recv()
+
+        @pl.when(lower)
+        def _():
+            for j in range(half):
+                soft_out[:, lanes(j * hp + i)] = os_in[j * hp + i]
+
+        @pl.when(upper)
+        def _():
+            for j in range(half):
+                lx_arrival(i, j).wait_recv()
                 ox_arrival(i, j).wait_recv()
-
-        def merge(j, carry):
-            def head(i, inner):
+            for j in range(half):
                 h = j * hp + i
-                gap = lx_in[j, pl.ds(i, 1), :] - ls_in[j, pl.ds(i, 1), :]
+                gap = lx_in[j, i, 0:1, :] - ls_in[j, i, 0:1, :]
                 gap = jnp.broadcast_to(gap, (tokens, tokens)).T
                 near = 1.0 / (1.0 + jnp.exp2(gap))
                 far = 1.0 / (1.0 + jnp.exp2(-gap))
-                mixed = near * os_in[:, lanes(h)].astype(F32)
-                mixed = mixed + far * ox_in[:, lanes(h)].astype(F32)
+                mixed = near * os_in[h].astype(F32) + far * ox_in[h].astype(F32)
                 soft_out[:, lanes(h)] = mixed.astype(BF16)
-                return inner
-
-            return lax.fori_loop(0, hp, head, carry, unroll=True)
-
-        lax.fori_loop(0, half, merge, 0)
-
-    for make in (en_copy, st_copy, pr_copy, ls_copy):
+
+        return carry
+
+    lax.fori_loop(0, hp, arrive, 0)
+
+    for make in (en_copy, st_copy, pr_copy):
         for d in others:
             make(d).wait_send()
-    for make in (k_copy, v_copy, q_copy, os_copy):
+    for make in (k_copy, v_copy, q_copy, os_copy, ls_copy):
         for i in range(hp):
             for d in others:
                 make(i, d).wait_send()
@@ -383,8 +386,8 @@
     def _():
         tot_copy().wait_send()
         for j in range(half):
-            lx_copy(j).wait_send()
             for i in range(hp):
+                lx_copy(i, j).wait_send()
                 ox_copy(i, j).wait_send()
 
 
@@ -574,25 +577,24 @@
     heads = log_decay.shape[1]
     half = n // 2
     hp = heads // half
-    width = hp * HEAD_DIM
-    level_rows = -(-hp // 8) * 8
     vmem = pl.BlockSpec(memory_space=pltpu.VMEM)
     far = pl.BlockSpec(memory_space=pltpu.HBM)
-    big = pltpu.VMEM((half * tokens, width), BF16)
+    big = pltpu.VMEM((hp, half * tokens, HEAD_DIM), BF16)
+    pieces = pltpu.VMEM((heads, tokens, HEAD_DIM), BF16)
     full = pltpu.VMEM((tokens, columns), BF16)
-    level = pltpu.VMEM((half, level_rows, tokens), F32)
+    level = pltpu.VMEM((half, hp, 8, tokens), F32)
     grid_states = pltpu.VMEM((half, hp, HEAD_DIM, HEAD_DIM), BF16)
     some_states = pltpu.VMEM((hp, HEAD_DIM, HEAD_DIM), BF16)
     dma = pltpu.SemaphoreType.DMA
     ring = [dma((half,)), dma((half,))]
     square = [dma((hp, half)), dma((hp, half))]
     single = [dma, dma]
-    return pl.pallas_call(
+    both = pl.pallas_call(
         functools.partial(kernel, n),
-        out_shape=[jax.ShapeDtypeStruct((tokens, columns), BF16)] * 2,
+        out_shape=jax.ShapeDtypeStruct((2, tokens, columns), BF16),
         in_specs=[far] * 3 + [vmem] + [far] * 3,
-        out_specs=[vmem] * 2,
-        scratch_shapes=[full] * 3 + [big] * 6 + [full] * 2 + [level] * 4
+        out_specs=vmem,
+        scratch_shapes=[full] * 3 + [big] * 6 + [pieces] * 2 + [level] * 4
         + [
             pltpu.VMEM((heads, HEAD_DIM, HEAD_DIM), BF16),
             grid_states,
@@ -604,9 +606,9 @@
             some_states,
             pltpu.VMEM((heads, tokens), F32),
             pltpu.VMEM((tokens, columns), F32),
-            dma((6,)),
+            dma((3 + 3 * hp,)),
         ]
-        + square * 4 + ring * 2 + single + ring + square + ring + square + ring,
+        + square * 4 + ring * 2 + single + ring + square * 4,
         compiler_params=pltpu.CompilerParams(
             collective_id=0, has_side_effects=True, vmem_limit_bytes=60 * 1024 * 1024
         ),
@@ -614,6 +616,7 @@
             flops=3 * 10**9, bytes_accessed=4 * 10**6, transcendentals=3 * 10**6
         ),
     )(lin_query, lin_key, lin_value, log_decay.T, soft_query, soft_key, soft_value)
+    return both[0], both[1]
 
 
 def solution(mesh):

time: 62.4 us -> 63.9 us (1.024)
  Pallas kernels: 58.2 us -> 60.3 us
    unnamed x4 -> x0, local copies, waits for them, and re-layouts: 2.74 us -> none
    squeeze x0 -> x1, local copies, waits for them, and re-layouts: none -> 2.28 us  [shards(): return (both[0], both[1])]
    pallas_call x1, Pallas kernels: 58.2 us -> 60.3 us  [shards(): pl.pallas_call(functools.partial(kernel, n), out_shape=jax.ShapeDtypeStru...]
where the time goes in v4:
time: 63.9 us; the launch traced here: 63.3 us
  Pallas kernels  60.3 us (94%)
  local copies, waits for them, and re-layouts  2.28 us (4%)
  between operations  0.64 us (1%)
    pallas_call x1, Pallas kernels, shards(): pl.pallas_call(functools.partial(kernel, n), out_shape=jax.ShapeDtypeStru...  60.3 us
    squeeze x1, local copies, waits for them, and re-layouts, shards(): return (both[0], both[1])  2.28 us

profile of v4, /device:TPU:10, one launch (start us, length us, event | category | flops | bytes accessed | tf_op | source)
XLA Modules:
  0.0 63.3 jit_solution(13978331802189394646)
XLA Ops:
  0.6 60.3 %shard_map.86 = bf16[2,128,2048]{2,1,0:T(8,128)(2,1)} custom-call(bf16[128,2048]{1,0:T(8,128)(2,1)} %lq_far.1, bf16[128,2048]{1,0:T(8,128)(2,1)} %lk_far.1, bf16[128,2048]{1,0:T(8,128)(2,1)} %lv_far.1, f32[16,128]{1,0:T(8,128)} %bitcast.5, bf16[128,2048]{1,0:T(8,128)(2,1)} %sq.1, bf16[128,2048]{1,0:T(8,128)(2,1)} %sk.1, bf16[128,2048]{1,0:T(8,128)(2,1)} %sv.1), custom_call_target="tpu_custom_call" | custom-call | flops 3000000000 | bytes 4000000 | tf_op jit(solution)/shard_map/pallas_call | solution.py:592
  61.0 2.3 %slice_bitcast_fusion = (bf16[128,2048]{1,0:T(8,128)(2,1)}, bf16[128,2048]{1,0:T(8,128)(2,1)}) fusion(bf16[2,128,2048]{2,1,0:T(8,128)(2,1)} %shard_map.86), kind=kLoop, calls=%fused_computation | loop fusion | bytes 2097152 | tf_op jit(solution)/shard_map/squeeze | solution.py:619

commit v5 on v3

--- a/solution.py
+++ b/solution.py
@@ -26,7 +26,7 @@
 def kernel(
     n,
     lq_far, lk_far, lv_far, ld, sq, sk, sv,
-    lin_out, soft_out,
+    both_out,
     lq, lk, lv, qs, ks, vs, qx, os, ox, os_in, ox_in, ls, lx, ls_in, lx_in,
     st, st_in, ends, ends_in, pr, pr_in, tot, tot_in, rst, inside,
     own_sem,
@@ -36,6 +36,7 @@
 ):
     tokens = lq.shape[0]
     heads = ld.shape[0]
+    lin_out, soft_out = both_out.at[0], both_out.at[1]
     half = n // 2
     hp = heads // half
     width = hp * HEAD_DIM
@@ -43,6 +44,11 @@
     side = me // half
     r = lax.rem(me, half)
     lower = side == 0
+    pair = me // 2
+    spot = lax.rem(me, 2)
+    partner = me + 1 - 2 * spot
+    pairs = n // 2
+    hh = heads // 2
     upper = side == 1
 
     def peer(d):
@@ -96,21 +102,20 @@
             qx_snd.at[i, d], qx_rcv.at[i, d], j,
         )
 
-    def st_copy(d):
-        j = peer(d)
-        return remote(
-            st.at[pl.ds(j * hp, hp)], st_in.at[r], st_snd.at[d], st_rcv.at[d], here(j)
-        )
-
-    def en_copy(d):
-        return remote(ends, ends_in.at[r], en_snd.at[d], en_rcv.at[d], here(peer(d)))
+    def st_copy():
+        return remote(st.at[pl.ds((1 - spot) * hh, hh)], st_in, st_snd, st_rcv, partner)
+
+    def en_copy():
+        return remote(ends, ends_in, en_snd, en_rcv, partner)
 
     def tot_copy():
-        return remote(tot, tot_in, tot_snd, tot_rcv, half + r)
-
-    def pr_copy(d):
-        j = peer(d)
-        return remote(pr.at[j], pr_in.at[r], pr_snd.at[d], pr_rcv.at[d], here(j))
+        return remote(tot, tot_in, tot_snd, tot_rcv, lax.rem(me + 2, n))
+
+    def pr_copy():
+        return remote(pr, pr_in.at[pl.ds(spot * hh, hh)], pr_snd, pr_rcv, partner)
+
+    def pr_arrival():
+        return remote(pr, pr_in.at[pl.ds((1 - spot) * hh, hh)], pr_snd, pr_rcv, partner)
 
     def os_copy(i, d):
         j = peer(d)
@@ -204,9 +209,8 @@
         return carry
 
     lax.fori_loop(0, heads, states, 0, unroll=4)
-    for d in others:
-        en_copy(d).start()
-        st_copy(d).start()
+    en_copy().start()
+    st_copy().start()
     lax.fori_loop(first, hp, spread_head, 0)
 
     def within(h, carry):
@@ -231,6 +235,44 @@
         level = jnp.broadcast_to(peak + jnp.log2(mass), (tokens, tokens)).T
         return result.astype(BF16), level[0:1, :]
 
+    def priors():
+        en_copy().wait_recv()
+        st_copy().wait_recv()
+
+        @pl.when(pair > 0)
+        def _():
+            tot_copy().wait_recv()
+
+        @pl.when(pair == 0)
+        def _():
+            tot_in[...] = jnp.zeros_like(tot_in)
+
+        first_here = spot == 0
+
+        def one(i, carry):
+            h = spot * hh + i
+            enter = tot_in[i].astype(F32)
+            mine = st[h].astype(F32)
+            theirs = st_in[i].astype(F32)
+            keep_mine = jnp.exp(ends[pl.ds(h, 1), :])
+            keep_theirs = jnp.exp(ends_in[pl.ds(h, 1), :])
+            early = jnp.where(first_here, mine, theirs)
+            late = jnp.where(first_here, theirs, mine)
+            middle = jnp.where(first_here, keep_mine, keep_theirs) * enter + early
+            leave = jnp.where(first_here, keep_theirs, keep_mine) * middle + late
+            tot[i] = leave.astype(BF16)
+            pr[i] = jnp.where(first_here, middle, enter).astype(BF16)
+            pr_in[h] = jnp.where(first_here, enter, middle).astype(BF16)
+            return carry
+
+        lax.fori_loop(0, hh, one, 0, unroll=2)
+
+        @pl.when(pair < pairs - 1)
+        def _():
+            tot_copy().start()
+
+        pr_copy().start()
+
     def head_step(i, carry):
         for d in others:
             k_copy(i, d).wait_recv()
@@ -260,41 +302,17 @@
             ls[b, pl.ds(i, 1), :] = level
         for d in others:
             os_copy(i, d).start()
+
+        @pl.when(i == jnp.minimum(pair, hp - 1))
+        def _():
+            priors()
+
         return carry
-
-    def priors():
-        for d in others:
-            en_copy(d).wait_recv()
-            st_copy(d).wait_recv()
-
-        st_in[r] = st[pl.ds(r * hp, hp)]
-        ends_in[r] = ends[...]
-
-        def one(i, carry):
-            state = jnp.where(upper, tot_in[i].astype(F32), 0.0)
-            for c in range(half):
-                pr[c, i] = state.astype(BF16)
-                keep = jnp.exp(ends_in[c, pl.ds(r * hp + i, 1), :])
-                state = keep * state + st_in[c, i].astype(F32)
-            tot[i] = state.astype(BF16)
-            return carry
-
-        lax.fori_loop(0, hp, one, 0, unroll=2)
 
     for copy in own[3:]:
         copy.wait()
 
-    lax.fori_loop(0, first, head_step, 0)
-
-    @pl.when(lower)
-    def _():
-        tot_in[...] = jnp.zeros_like(tot_in)
-        priors()
-        tot_copy().start()
-        for d in others:
-            pr_copy(d).start()
-
-    lax.fori_loop(first, hp, head_step, 0)
+    lax.fori_loop(0, hp, head_step, 0)
 
     @pl.when(lower)
     def _():
@@ -304,27 +322,18 @@
     for d in others:
         ls_copy(d).start()
 
-    @pl.when(upper)
-    def _():
-        tot_copy().wait_recv()
-        priors()
-        for d in others:
-            pr_copy(d).start()
-
     lax.fori_loop(0, heads, within, 0, unroll=4)
-    pr_in[r] = pr[r]
     os_in[:, cols(r)] = os[rows(r), :]
     ls_in[r] = ls[r]
 
-    for d in others:
-        pr_copy(d).wait_recv()
+    pr_arrival().wait_recv()
 
     def finish(j, carry):
         def head(i, inner):
             h = j * hp + i
             down = jnp.broadcast_to(rst[pl.ds(h, 1), :], (tokens, tokens)).T
             scaled = (lq[:, lanes(h)].astype(F32) * jnp.exp(down)).astype(BF16)
-            total = inside[:, lanes(h)] + contract(scaled, pr_in[j, i], ((1,), (0,)))
+            total = inside[:, lanes(h)] + contract(scaled, pr_in[h], ((1,), (0,)))
             norm = lax.rsqrt(jnp.mean(total * total, axis=1, keepdims=True) + NORM_EPS)
             lin_out[:, lanes(h)] = (total * norm).astype(BF16)
             return inner
@@ -365,9 +374,15 @@
 
         lax.fori_loop(0, half, merge, 0)
 
-    for make in (en_copy, st_copy, pr_copy, ls_copy):
-        for d in others:
-            make(d).wait_send()
+    for make in (en_copy, st_copy, pr_copy):
+        make().wait_send()
+    for d in others:
+        ls_copy(d).wait_send()
+
+    @pl.when(pair < pairs - 1)
+    def _():
+        tot_copy().wait_send()
+
     for make in (k_copy, v_copy, q_copy, os_copy):
         for i in range(hp):
             for d in others:
@@ -381,7 +396,6 @@
 
     @pl.when(lower)
     def _():
-        tot_copy().wait_send()
         for j in range(half):
             lx_copy(j).wait_send()
             for i in range(hp):
@@ -581,32 +595,31 @@
     big = pltpu.VMEM((half * tokens, width), BF16)
     full = pltpu.VMEM((tokens, columns), BF16)
     level = pltpu.VMEM((half, level_rows, tokens), F32)
-    grid_states = pltpu.VMEM((half, hp, HEAD_DIM, HEAD_DIM), BF16)
-    some_states = pltpu.VMEM((hp, HEAD_DIM, HEAD_DIM), BF16)
+    some_states = pltpu.VMEM((heads // 2, HEAD_DIM, HEAD_DIM), BF16)
     dma = pltpu.SemaphoreType.DMA
     ring = [dma((half,)), dma((half,))]
     square = [dma((hp, half)), dma((hp, half))]
     single = [dma, dma]
-    return pl.pallas_call(
+    both = pl.pallas_call(
         functools.partial(kernel, n),
-        out_shape=[jax.ShapeDtypeStruct((tokens, columns), BF16)] * 2,
+        out_shape=jax.ShapeDtypeStruct((2, tokens, columns), BF16),
         in_specs=[far] * 3 + [vmem] + [far] * 3,
-        out_specs=[vmem] * 2,
+        out_specs=vmem,
         scratch_shapes=[full] * 3 + [big] * 6 + [full] * 2 + [level] * 4
         + [
             pltpu.VMEM((heads, HEAD_DIM, HEAD_DIM), BF16),
-            grid_states,
+            some_states,
             pltpu.VMEM((heads, tokens), F32),
-            pltpu.VMEM((half, heads, tokens), F32),
-            grid_states,
-            grid_states,
+            pltpu.VMEM((heads, tokens), F32),
+            some_states,
+            pltpu.VMEM((heads, HEAD_DIM, HEAD_DIM), BF16),
             some_states,
             some_states,
             pltpu.VMEM((heads, tokens), F32),
             pltpu.VMEM((tokens, columns), F32),
             dma((6,)),
         ]
-        + square * 4 + ring * 2 + single + ring + square + ring + square + ring,
+        + square * 4 + single * 4 + square + ring + square + ring,
         compiler_params=pltpu.CompilerParams(
             collective_id=0, has_side_effects=True, vmem_limit_bytes=60 * 1024 * 1024
         ),
@@ -614,6 +627,7 @@
             flops=3 * 10**9, bytes_accessed=4 * 10**6, transcendentals=3 * 10**6
         ),
     )(lin_query, lin_key, lin_value, log_decay.T, soft_query, soft_key, soft_value)
+    return both[0], both[1]
 
 
 def solution(mesh):

time: 62.4 us -> 68 us (1.090)
  the two profiles are of different devices: /device:TPU:10 before, /device:TPU:26 now
where the time goes in v5:
time: 68 us; the launch traced here: 67.7 us
  Pallas kernels  64.8 us (95%)
  local copies, waits for them, and re-layouts  2.28 us (3%)
    pallas_call x1, Pallas kernels, shards(): pl.pallas_call(functools.partial(kernel, n), out_shape=jax.ShapeDtypeStru...  64.8 us
    squeeze x1, local copies, waits for them, and re-layouts, shards(): return (both[0], both[1])  2.28 us

profile of v5, /device:TPU:26, one launch (start us, length us, event | category | flops | bytes accessed | tf_op | source)
XLA Modules:
  0.0 67.7 jit_solution(15381976278920651023)
XLA Ops:
  0.6 64.8 %shard_map.86 = bf16[2,128,2048]{2,1,0:T(8,128)(2,1)} custom-call(bf16[128,2048]{1,0:T(8,128)(2,1)} %lq_far.1, bf16[128,2048]{1,0:T(8,128)(2,1)} %lk_far.1, bf16[128,2048]{1,0:T(8,128)(2,1)} %lv_far.1, f32[16,128]{1,0:T(8,128)} %bitcast.5, bf16[128,2048]{1,0:T(8,128)(2,1)} %sq.1, bf16[128,2048]{1,0:T(8,128)(2,1)} %sk.1, bf16[128,2048]{1,0:T(8,128)(2,1)} %sv.1), custom_call_target="tpu_custom_call" | custom-call | flops 3000000000 | bytes 4000000 | tf_op jit(solution)/shard_map/pallas_call | solution.py:603
  65.5 2.3 %slice_bitcast_fusion = (bf16[128,2048]{1,0:T(8,128)(2,1)}, bf16[128,2048]{1,0:T(8,128)(2,1)}) fusion(bf16[2,128,2048]{2,1,0:T(8,128)(2,1)} %shard_map.86), kind=kLoop, calls=%fused_computation | loop fusion | bytes 2097152 | tf_op jit(solution)/shard_map/squeeze | solution.py:630

commit v6 on v5

--- a/solution.py
+++ b/solution.py
@@ -274,6 +274,10 @@
         pr_copy().start()
 
     def head_step(i, carry):
+        @pl.when(i == jnp.minimum(pair, hp - 1))
+        def _():
+            priors()
+
         for d in others:
             k_copy(i, d).wait_recv()
             v_copy(i, d).wait_recv()
@@ -302,10 +306,6 @@
             ls[b, pl.ds(i, 1), :] = level
         for d in others:
             os_copy(i, d).start()
-
-        @pl.when(i == jnp.minimum(pair, hp - 1))
-        def _():
-            priors()
 
         return carry
 

time: 68 us -> 72.2 us (1.062)
  Pallas kernels: 64.8 us -> 69 us
    pallas_call x1, Pallas kernels: 64.8 us -> 69 us  [shards(): pl.pallas_call(functools.partial(kernel, n), out_shape=jax.ShapeDtypeStru...]
where the time goes in v6:
time: 72.2 us; the launch traced here: 72 us
  Pallas kernels  69 us (96%)
  local copies, waits for them, and re-layouts  2.28 us (3%)
    pallas_call x1, Pallas kernels, shards(): pl.pallas_call(functools.partial(kernel, n), out_shape=jax.ShapeDtypeStru...  69 us
    squeeze x1, local copies, waits for them, and re-layouts, shards(): return (both[0], both[1])  2.28 us

profile of v6, /device:TPU:26, one launch (start us, length us, event | category | flops | bytes accessed | tf_op | source)
XLA Modules:
  0.0 72.0 jit_solution(12831788089618486462)
XLA Ops:
  0.6 69.0 %shard_map.86 = bf16[2,128,2048]{2,1,0:T(8,128)(2,1)} custom-call(bf16[128,2048]{1,0:T(8,128)(2,1)} %lq_far.1, bf16[128,2048]{1,0:T(8,128)(2,1)} %lk_far.1, bf16[128,2048]{1,0:T(8,128)(2,1)} %lv_far.1, f32[16,128]{1,0:T(8,128)} %bitcast.5, bf16[128,2048]{1,0:T(8,128)(2,1)} %sq.1, bf16[128,2048]{1,0:T(8,128)(2,1)} %sk.1, bf16[128,2048]{1,0:T(8,128)(2,1)} %sv.1), custom_call_target="tpu_custom_call" | custom-call | flops 3000000000 | bytes 4000000 | tf_op jit(solution)/shard_map/pallas_call | solution.py:603
  69.7 2.3 %slice_bitcast_fusion = (bf16[128,2048]{1,0:T(8,128)(2,1)}, bf16[128,2048]{1,0:T(8,128)(2,1)}) fusion(bf16[2,128,2048]{2,1,0:T(8,128)(2,1)} %shard_map.86), kind=kLoop, calls=%fused_computation | loop fusion | bytes 2097152 | tf_op jit(solution)/shard_map/squeeze | solution.py:630
